TPU v7x, 32 devices: a whole 2x2x4 slice. The times are simulated.
32 devices in a mesh: dp: 8 (over z, x), rep: 4 (over y, core).
Axes of the slice: x: 2, y: 2, z: 4, core: 2. Of those that a mesh axis runs over, the one named last changes fastest.
Arguments:
- content_stream: bfloat16 [32, 512, 768], P(('dp', 'rep')), may hold values from -6 to 6
- query_stream: bfloat16 [32, 512, 768], P(('dp', 'rep')), may hold values from -6 to 6
- segments: int32 [32, 512], P(('dp', 'rep')), may hold values from 0 to 6, never falling along the last dimension, each value on 1 to 192 neighbouring positions
- perm_order: int32 [32, 512], P(('dp', 'rep')), may hold values from 0 to 511, each once within a row
- predicted: int32 [32, 512], P(('dp', 'rep')), may hold values 0 or 1
- buckets: int32 [1023], replicated, may hold values from 0 to 31, as said below
- bias_table: bfloat16 [32, 12], replicated, may hold values from -4 to 4
- project_one: bfloat16 [768, 2304], P('dp', 'rep'), may hold values from -0.21875 to 0.21875
- output_one: bfloat16 [768, 768], P('dp', 'rep'), may hold values from -1.75 to 1.75
- expand_one: bfloat16 [768, 3072], P('dp', 'rep'), may hold values from -0.21875 to 0.21875
- contract_one: bfloat16 [3072, 768], P('dp', 'rep'), may hold values from -0.109375 to 0.109375
- vectors_one: bfloat16 [12, 768], P('rep', 'dp'), may hold values from -2 to 2, as said below
- project_two: bfloat16 [768, 2304], P('dp', 'rep'), may hold values from -0.21875 to 0.21875
- output_two: bfloat16 [768, 768], P('dp', 'rep'), may hold values from -1.75 to 1.75
- expand_two: bfloat16 [768, 3072], P('dp', 'rep'), may hold values from -0.21875 to 0.21875
- contract_two: bfloat16 [3072, 768], P('dp', 'rep'), may hold values from -0.109375 to 0.109375
- vectors_two: bfloat16 [12, 768], P('rep', 'dp'), may hold values from -2 to 2, as said below
- content_cotangent: bfloat16 [32, 512, 768], P(('dp', 'rep')), may hold values from -6 to 6
- query_cotangent: bfloat16 [32, 512, 768], P(('dp', 'rep')), may hold values from -6 to 6
Outputs:
- content_result: bfloat16 [32, 512, 768], P(('dp', 'rep'))
- query_result: bfloat16 [32, 512, 768], P(('dp', 'rep'))
- content_gradient: float32 [32, 512, 768], P(('dp', 'rep'))
- query_gradient: float32 [32, 512, 768], P(('dp', 'rep'))
- table_gradient: float32 [32, 12], replicated
- project_one_gradient: float32 [768, 2304], P('dp', 'rep')
- output_one_gradient: float32 [768, 768], P('dp', 'rep')
- expand_one_gradient: float32 [768, 3072], P('dp', 'rep')
- contract_one_gradient: float32 [3072, 768], P('dp', 'rep')
- vectors_one_gradient: float32 [12, 768], P('rep', 'dp')
- project_two_gradient: float32 [768, 2304], P('dp', 'rep')
- output_two_gradient: float32 [768, 768], P('dp', 'rep')
- expand_two_gradient: float32 [768, 3072], P('dp', 'rep')
- contract_two_gradient: float32 [3072, 768], P('dp', 'rep')
- vectors_two_gradient: float32 [12, 768], P('rep', 'dp')
Inputs may be any that keep to these rules, and one draw needn't show every extreme that they name: `segments`: in each row segment numbers never fall; 6 marks the padding at the row's end, the numbers below it are documents. `perm_order`: each row is a permutation of 0 to 511; within a document a smaller number comes earlier in the permuted order. `buckets`: entry 511 + d is the bucket of relative position d (key minus query): 0 at d = 0, at most 15 for d < 0, 16 or more for d > 0, never falling as the magnitude grows on either side. `vectors_one`: rows 3 and 6 lie near 1. `vectors_two`: rows 3 and 6 lie near 1.
All inputs are finite; a program needn't handle non-finite values. No bound on the sum of `predicted` on one device may be relied on, other than what follows from the above.
Results may differ from a plain program's by a relative error of at most 0.023.
Values may be sent and summed in bfloat16 or wider, within the bound.
A program may use at most 320 MiB of HBM per device.

v0:
```python
import jax
import jax.numpy as jnp
from jax import lax
from jax.sharding import PartitionSpec as P

H = 12
HD = 64
ROW = 512
DOCS = 6


def layer_norm(values, gain, shift):
    centered = values - jnp.mean(values, axis=-1, keepdims=True)
    spread = jnp.mean(centered * centered, axis=-1, keepdims=True)
    return centered * lax.rsqrt(spread + 1e-05) * gain + shift


def exact_gelu(values):
    return jax.nn.gelu(values, approximate=False)


def fetch_weights(project, output, expand, contract, vectors):
    partial_set = (
        lax.all_gather(project, "rep", axis=1, tiled=True),
        lax.all_gather(output, "rep", axis=1, tiled=True),
        lax.all_gather(expand, "rep", axis=1, tiled=True),
        lax.all_gather(contract, "rep", axis=1, tiled=True),
        lax.all_gather(vectors, "rep", axis=0, tiled=True),
    )
    return (
        lax.all_gather(partial_set[0], "dp", axis=0, tiled=True),
        lax.all_gather(partial_set[1], "dp", axis=0, tiled=True),
        lax.all_gather(partial_set[2], "dp", axis=0, tiled=True),
        lax.all_gather(partial_set[3], "dp", axis=0, tiled=True),
        lax.all_gather(partial_set[4], "dp", axis=1, tiled=True),
    )


def push_gradients(gradients):
    partial_set = (
        lax.psum_scatter(
            gradients[0].astype(jnp.bfloat16), "rep", scatter_dimension=1, tiled=True
        ).astype(jnp.float32),
        lax.psum_scatter(
            gradients[1].astype(jnp.bfloat16), "rep", scatter_dimension=1, tiled=True
        ).astype(jnp.float32),
        lax.psum_scatter(
            gradients[2].astype(jnp.bfloat16), "rep", scatter_dimension=1, tiled=True
        ).astype(jnp.float32),
        lax.psum_scatter(
            gradients[3].astype(jnp.bfloat16), "rep", scatter_dimension=1, tiled=True
        ).astype(jnp.float32),
        lax.psum_scatter(
            gradients[4].astype(jnp.bfloat16), "rep", scatter_dimension=0, tiled=True
        ).astype(jnp.float32),
    )
    return (
        lax.psum_scatter(partial_set[0], "dp", scatter_dimension=0, tiled=True),
        lax.psum_scatter(partial_set[1], "dp", scatter_dimension=0, tiled=True),
        lax.psum_scatter(partial_set[2], "dp", scatter_dimension=0, tiled=True),
        lax.psum_scatter(partial_set[3], "dp", scatter_dimension=0, tiled=True),
        lax.psum_scatter(partial_set[4], "dp", scatter_dimension=1, tiled=True),
    )


def toeplitz_rows(per_offset, length):
    heads = per_offset.shape[0]
    period = 2 * length - 1
    tiled = jnp.tile(per_offset, (1, length))
    window = tiled[:, length - 1 : length - 1 + length * (period - 1)]
    return window.reshape(heads, length, period - 1)[:, :, :length]


def diagonal_sums(grid):
    heads, length = (grid.shape[0], grid.shape[1])
    period = 2 * length - 1
    padded = jnp.concatenate([grid, jnp.zeros((heads, length, length - 2), grid.dtype)], axis=2)
    flat = padded.reshape(heads, length * (period - 1))
    placed = jnp.concatenate(
        [jnp.zeros((heads, length - 1), grid.dtype), flat, jnp.zeros((heads, 1), grid.dtype)],
        axis=1,
    )
    return jnp.sum(placed.reshape(heads, length, period), axis=1)


def score_block(queries, keys, allowed, position_bias):
    scores = (
        jnp.einsum("qhd,khd->hqk", queries, keys, preferred_element_type=jnp.float32) * 0.125
        + position_bias
    )
    return jnp.where(allowed, scores, -1e30)


def attend(bundle, position_bias):
    queries, keys, values, allowed = bundle
    scores = score_block(queries, keys, allowed, position_bias)
    row_max = jnp.max(scores, axis=-1, keepdims=True)
    lifted = jnp.where(allowed, jnp.exp(scores - row_max), 0.0)
    row_total = jnp.sum(lifted, axis=-1, keepdims=True)
    row_total = jnp.where(row_total > 0, row_total, 1.0)
    chances = (lifted / row_total).astype(jnp.bfloat16)
    context = jnp.einsum("hqk,khd->qhd", chances, values, preferred_element_type=jnp.float32)
    return (context.astype(jnp.bfloat16), row_max, row_total)


def attend_backward(grid_total, bundle, position_bias):
    queries, keys, values, allowed, row_max, row_total, grad_context = bundle
    scores = score_block(queries, keys, allowed, position_bias)
    chances = jnp.where(allowed, jnp.exp(scores - row_max), 0.0) / row_total
    chances_low = chances.astype(jnp.bfloat16)
    grad_values = jnp.einsum(
        "hqk,qhd->khd", chances_low, grad_context, preferred_element_type=jnp.float32
    )
    grad_chances = jnp.einsum(
        "qhd,khd->hqk", grad_context, values, preferred_element_type=jnp.float32
    )
    grad_scores = chances * (grad_chances - jnp.sum(chances * grad_chances, axis=-1, keepdims=True))
    scores_low = grad_scores.astype(jnp.bfloat16)
    grad_queries = (
        jnp.einsum("hqk,khd->qhd", scores_low, keys, preferred_element_type=jnp.float32) * 0.125
    )
    grad_keys = (
        jnp.einsum("hqk,qhd->khd", scores_low, queries, preferred_element_type=jnp.float32) * 0.125
    )
    return (grid_total + scores_low.astype(jnp.float32), (grad_queries, grad_keys, grad_values))


def forward_layer(content_rows, query_rows, weights, position_bias, allowed_content, allowed_query):
    project, output, expand, contract, vectors = weights
    width = project.shape[0]
    count = content_rows.shape[0]
    vector_rows = vectors.astype(jnp.float32)
    mixed = jnp.dot(content_rows, project, preferred_element_type=jnp.float32)
    queries_content = (mixed[:, :width] + vector_rows[0]).astype(jnp.bfloat16)
    keys = mixed[:, width : 2 * width].astype(jnp.bfloat16)
    values = (mixed[:, 2 * width :] + vector_rows[1]).astype(jnp.bfloat16)
    queries_query = (
        jnp.dot(query_rows, project[:, :width], preferred_element_type=jnp.float32) + vector_rows[0]
    ).astype(jnp.bfloat16)
    shape = (-1, ROW, H, HD)

    def passed(queries, allowed):
        bundles = (queries.reshape(shape), keys.reshape(shape), values.reshape(shape), allowed)
        return lax.map(lambda bundle: attend(bundle, position_bias), bundles)

    context_content, max_content, total_content = passed(queries_content, allowed_content)
    context_query, max_query, total_query = passed(queries_query, allowed_query)
    inputs = jnp.concatenate([content_rows, query_rows], axis=0)
    context = jnp.concatenate(
        [context_content.reshape(-1, width), context_query.reshape(-1, width)], axis=0
    )
    attended = jnp.dot(context, output, preferred_element_type=jnp.float32) + vector_rows[2]
    first_sum = inputs.astype(jnp.float32) + attended
    normed = layer_norm(first_sum, vector_rows[3], vector_rows[4])
    normed_low = normed.astype(jnp.bfloat16)
    hidden = jnp.dot(normed_low, expand, preferred_element_type=jnp.float32) + vector_rows[
        8:
    ].reshape(-1)
    activated = exact_gelu(hidden).astype(jnp.bfloat16)
    feed_out = jnp.dot(activated, contract, preferred_element_type=jnp.float32) + vector_rows[5]
    second_sum = normed + feed_out
    result = layer_norm(second_sum, vector_rows[6], vector_rows[7]).astype(jnp.bfloat16)
    kept = (inputs, context, first_sum, normed_low, hidden, activated, second_sum)
    saved = (
        queries_content,
        queries_query,
        keys,
        values,
        max_content,
        total_content,
        max_query,
        total_query,
        kept,
    )
    return (result[:count], result[count:], saved)


def branch_backward(grad_result, kept, weights):
    project, output, expand, contract, vectors = weights
    vector_rows = vectors.astype(jnp.float32)
    inputs, context, first_sum, normed_low, hidden, activated, second_sum = kept
    unused, second_back = jax.vjp(layer_norm, second_sum, vector_rows[6], vector_rows[7])
    grad_second, grad_gain_two, grad_shift_two = second_back(grad_result)
    grad_feed = grad_second.astype(jnp.bfloat16)
    grad_contract = jnp.einsum(
        "tf,td->fd", activated, grad_feed, preferred_element_type=jnp.float32
    )
    grad_active = jnp.einsum("td,fd->tf", grad_feed, contract, preferred_element_type=jnp.float32)
    unused, gelu_back = jax.vjp(exact_gelu, hidden)
    grad_hidden = gelu_back(grad_active)[0].astype(jnp.bfloat16)
    grad_expand = jnp.einsum(
        "td,tf->df", normed_low, grad_hidden, preferred_element_type=jnp.float32
    )
    grad_normed = grad_second + jnp.einsum(
        "tf,df->td", grad_hidden, expand, preferred_element_type=jnp.float32
    )
    unused, first_back = jax.vjp(layer_norm, first_sum, vector_rows[3], vector_rows[4])
    grad_first, grad_gain_one, grad_shift_one = first_back(grad_normed)
    grad_attended = grad_first.astype(jnp.bfloat16)
    grad_output = jnp.einsum(
        "te,td->ed", context, grad_attended, preferred_element_type=jnp.float32
    )
    grad_context = jnp.einsum(
        "td,ed->te", grad_attended, output, preferred_element_type=jnp.float32
    ).astype(jnp.bfloat16)
    small = (
        jnp.sum(grad_attended, axis=0, dtype=jnp.float32),
        grad_gain_one,
        grad_shift_one,
        jnp.sum(grad_feed, axis=0, dtype=jnp.float32),
        grad_gain_two,
        grad_shift_two,
        jnp.sum(grad_hidden, axis=0, dtype=jnp.float32),
    )
    return (grad_first, grad_context, (grad_output, grad_expand, grad_contract), small)


def backward_layer(
    grad_content,
    grad_query,
    saved,
    weights,
    position_bias,
    allowed_content,
    allowed_query,
    grid_total,
):
    project = weights[0]
    width = project.shape[0]
    (
        queries_content,
        queries_query,
        keys,
        values,
        max_content,
        total_content,
        max_query,
        total_query,
        kept,
    ) = saved
    count = grad_content.shape[0]
    both_rows = kept[0]
    content_rows = both_rows[:count]
    grad_both = jnp.concatenate([grad_content, grad_query], axis=0)
    grad_first, grad_context, mats, small = branch_backward(grad_both, kept, weights)
    shape = (-1, ROW, H, HD)

    def passed(total, queries, allowed, row_max, row_total, context_grad):
        bundles = (
            queries.reshape(shape),
            keys.reshape(shape),
            values.reshape(shape),
            allowed,
            row_max,
            row_total,
            context_grad.reshape(shape),
        )
        return lax.scan(
            lambda carry, bundle: attend_backward(carry, bundle, position_bias), total, bundles
        )

    grid_total, (dq_content, dk_content, dv_content) = passed(
        grid_total,
        queries_content,
        allowed_content,
        max_content,
        total_content,
        grad_context[:count],
    )
    grid_total, (dq_query, dk_query, dv_query) = passed(
        grid_total, queries_query, allowed_query, max_query, total_query, grad_context[count:]
    )
    grad_keys = (dk_content + dk_query).reshape(-1, width).astype(jnp.bfloat16)
    grad_values = (dv_content + dv_query).reshape(-1, width).astype(jnp.bfloat16)
    grad_qcontent = dq_content.reshape(-1, width).astype(jnp.bfloat16)
    grad_qquery = dq_query.reshape(-1, width).astype(jnp.bfloat16)
    grad_queries_both = jnp.concatenate([grad_qcontent, grad_qquery], axis=0)
    grad_kv = jnp.concatenate([grad_keys, grad_values], axis=1)
    query_part = jnp.einsum(
        "td,te->de", both_rows, grad_queries_both, preferred_element_type=jnp.float32
    )
    kv_part = jnp.einsum("td,te->de", content_rows, grad_kv, preferred_element_type=jnp.float32)
    grad_project = jnp.concatenate([query_part, kv_part], axis=1)
    grad_mixed = jnp.concatenate([grad_qcontent, grad_kv], axis=1)
    input_content = grad_first[:count] + jnp.einsum(
        "te,de->td", grad_mixed, project, preferred_element_type=jnp.float32
    )
    input_query = grad_first[count:] + jnp.einsum(
        "te,de->td", grad_qquery, project[:, :width], preferred_element_type=jnp.float32
    )
    head_rows = jnp.stack(
        [
            jnp.sum(grad_queries_both, axis=0, dtype=jnp.float32),
            jnp.sum(grad_values, axis=0, dtype=jnp.float32),
            small[0],
            small[1],
            small[2],
            small[3],
            small[4],
            small[5],
        ]
    )
    grad_vectors = jnp.concatenate([head_rows, small[6].reshape(-1, width)], axis=0)
    gradients = (grad_project, mats[0], mats[1], mats[2], grad_vectors)
    return (input_content, input_query, gradients, grid_total)


def shards(
    content_stream,
    query_stream,
    segments,
    perm_order,
    predicted,
    buckets,
    bias_table,
    project_one,
    output_one,
    expand_one,
    contract_one,
    vectors_one,
    project_two,
    output_two,
    expand_two,
    contract_two,
    vectors_two,
    content_cotangent,
    query_cotangent,
):
    rows, length, width = content_stream.shape
    heads = bias_table.shape[1]
    same_doc = (segments[:, :, None] == segments[:, None, :]) & (segments[:, None, :] != DOCS)
    visible = predicted[:, None, :] == 0
    allowed_content = same_doc & (visible | (perm_order[:, None, :] <= perm_order[:, :, None]))
    allowed_query = same_doc & (visible | (perm_order[:, None, :] < perm_order[:, :, None]))
    selector = (
        buckets[:, None] == jnp.arange(bias_table.shape[0], dtype=jnp.int32)[None, :]
    ).astype(jnp.float32)
    per_offset = jnp.dot(selector, bias_table.astype(jnp.float32), precision=lax.Precision.HIGHEST)
    position_bias = toeplitz_rows(per_offset.T, length)
    weights_one = fetch_weights(project_one, output_one, expand_one, contract_one, vectors_one)
    middle_content, middle_query, saved_one = forward_layer(
        content_stream.reshape(-1, width),
        query_stream.reshape(-1, width),
        weights_one,
        position_bias,
        allowed_content,
        allowed_query,
    )
    weights_two = fetch_weights(project_two, output_two, expand_two, contract_two, vectors_two)
    result_content, result_query, saved_two = forward_layer(
        middle_content, middle_query, weights_two, position_bias, allowed_content, allowed_query
    )
    again_two = fetch_weights(project_two, output_two, expand_two, contract_two, vectors_two)
    grid_total = jnp.zeros((heads, length, length), jnp.float32)
    grad_mid_content, grad_mid_query, gradients_two, grid_total = backward_layer(
        content_cotangent.reshape(-1, width).astype(jnp.float32),
        query_cotangent.reshape(-1, width).astype(jnp.float32),
        saved_two,
        again_two,
        position_bias,
        allowed_content,
        allowed_query,
        grid_total,
    )
    shards_two = push_gradients(gradients_two)
    again_one = fetch_weights(project_one, output_one, expand_one, contract_one, vectors_one)
    grad_content, grad_query, gradients_one, grid_total = backward_layer(
        grad_mid_content,
        grad_mid_query,
        saved_one,
        again_one,
        position_bias,
        allowed_content,
        allowed_query,
        grid_total,
    )
    shards_one = push_gradients(gradients_one)
    distances = diagonal_sums(grid_total)
    table_local = jnp.dot(selector.T, distances.T, precision=lax.Precision.HIGHEST)
    table_gradient = lax.psum(table_local, ("dp", "rep"))
    return (
        result_content.reshape(rows, length, width),
        result_query.reshape(rows, length, width),
        grad_content.reshape(rows, length, width),
        grad_query.reshape(rows, length, width),
        table_gradient,
        shards_one[0],
        shards_one[1],
        shards_one[2],
        shards_one[3],
        shards_one[4],
        shards_two[0],
        shards_two[1],
        shards_two[2],
        shards_two[3],
        shards_two[4],
    )


def solution(mesh):
    in_specs = (
        P(("dp", "rep"), None, None),
        P(("dp", "rep"), None, None),
        P(("dp", "rep"), None),
        P(("dp", "rep"), None),
        P(("dp", "rep"), None),
        P(),
        P(),
        P("dp", "rep"),
        P("dp", "rep"),
        P("dp", "rep"),
        P("dp", "rep"),
        P("rep", "dp"),
        P("dp", "rep"),
        P("dp", "rep"),
        P("dp", "rep"),
        P("dp", "rep"),
        P("rep", "dp"),
        P(("dp", "rep"), None, None),
        P(("dp", "rep"), None, None),
    )
    out_specs = (
        P(("dp", "rep"), None, None),
        P(("dp", "rep"), None, None),
        P(("dp", "rep"), None, None),
        P(("dp", "rep"), None, None),
        P(),
        P("dp", "rep"),
        P("dp", "rep"),
        P("dp", "rep"),
        P("dp", "rep"),
        P("rep", "dp"),
        P("dp", "rep"),
        P("dp", "rep"),
        P("dp", "rep"),
        P("dp", "rep"),
        P("rep", "dp"),
    )
    return jax.shard_map(shards, mesh=mesh, in_specs=in_specs, out_specs=out_specs, check_vma=False)
```

profile of v0, /device:TPU:0, one launch (start us, length us, event | category | flops | bytes accessed | tf_op | source)
XLA Modules:
  0.0 1751.2 jit_solution(8953856904571093452)
XLA Ops:
  78.3 30.8 %all-gather.5 = bf16[8,96,12]{1,2,0:T(8,128)(2,1)S(1)} all-gather(bf16[1,96,12]{1,2,0:T(8,128)(2,1)S(1)} %bitcast.262), channel_id=1, replica_groups=mesh['dp'=8,'rep'=4] {'dp'}, dimensions={0}, use_global_device_ids=true | all-gather | bytes 20736 | tf_op jit(solution)/shard_map/all_gather | solution.py:35
  114.9 30.6 %all-gather.2 = bf16[8,96,12]{1,2,0:T(8,128)(2,1)S(1)} all-gather(bf16[1,96,12]{1,2,0:T(8,128)(2,1)S(1)} %bitcast.263), channel_id=1, replica_groups=mesh['dp'=8,'rep'=4] {'dp'}, dimensions={0}, use_global_device_ids=true | all-gather | bytes 20736 | tf_op jit(solution)/shard_map/all_gather | solution.py:35
  163.4 38.4 %tile.10 = f32[12,523776]{1,0:T(8,128)} reshape(f32[12,512,1023]{2,1,0:T(8,128)} %tile.4) | data formatting | bytes 50282496 | tf_op jit(solution)/shard_map/tile | solution.py:69
  201.8 25.7 %slice.176 = f32[12,523264]{1,0:T(8,128)} slice(f32[12,523776]{1,0:T(8,128)} %tile.10), slice={[0:12], [511:523775]} | slice | bytes 50233344 | tf_op jit(solution)/shard_map/slice | solution.py:70
  227.5 55.1 %reshape.534 = f32[12,512,1022]{2,1,0:T(8,128)} reshape(f32[12,523264]{1,0:T(8,128)} %slice.176) | data formatting | bytes 50233344 | tf_op jit(solution)/shard_map/reshape | solution.py:71
  358.4 38.5 %multiply_convert_fusion.5 = (bf16[1024,3072]{1,0:T(8,128)(2,1)}, f32[1024,3072]{1,0:T(8,128)}, f32[1024,3072]{1,0:T(8,128)}) fusion(f32[3072]{0:T(1024)S(1)} %add.363, bf16[768,3072]{1,0:T(8,128)(2,1)} %all-gather.19.cloned.1.call-done, f32[1024,768]{0,1:T(8,128)S(1)} %get-tuple-element.421, f32[768]{0:T(1024)S(1)} %get-tuple-element.377, ...), kind=kOutput, calls=%fused_computation.36 | convolution fusion | flops 5043388416 | bytes 39348224 | tf_op jit(solution)/shard_map/dot_general | solution.py:156
  476.6 38.1 %multiply_convert_fusion.4 = (bf16[1024,3072]{1,0:T(8,128)(2,1)}, f32[1024,3072]{1,0:T(8,128)}, f32[1024,3072]{1,0:T(8,128)}) fusion(f32[3072]{0:T(1024)S(1)} %copy-done.116, bf16[768,3072]{1,0:T(8,128)(2,1)} %all-gather.27.cloned.1.call-done, f32[1024,768]{0,1:T(8,128)S(1)} %get-tuple-element.430, f32[768]{0:T(1024)S(1)} %copy-done.128, ...), kind=kOutput, calls=%fused_computation.19 | convolution fusion | flops 5043388416 | bytes 39348224 | tf_op jit(solution)/shard_map/dot_general | solution.py:156
  514.7 43.1 %all-gather.29.cloned.1.call-done = bf16[3072,768]{0,1:T(8,128)(2,1)} async-done(((bf16[384,768]{0,1:T(8,128)(2,1)}), bf16[3072,768]{0,1:T(8,128)(2,1)}) %all-gather.29.cloned.1.call-update) | async-done | bytes 4718608 | tf_op jit(solution)/shard_map/all_gather | solution.py:34
  686.7 19.4 %fusion.155 = (bf16[3072]{0:T(1024)(128)(2,1)}, bf16[1024,3072]{1,0:T(8,128)(2,1)}) fusion(f32[1024,3072]{1,0:T(8,128)} %get-tuple-element.402, bf16[1024,768]{0,1:T(8,128)(2,1)S(1)} %get-tuple-element.389, bf16[3072,768]{0,1:T(8,128)(2,1)} %all-gather.21.cloned.1.call-done, f32[1024,3072]{1,0:T(8,128)} %get-tuple-element.422, f32[3072]{0:T(1024)S(1)} %copy-done.115), kind=kOutput, calls=%fused_computation.300 | convolution fusion | flops 4882166784 | bytes 37767168 | tf_op jit(solution)/shard_map/td,fd->tf/dot_general | solution.py:188
  758.5 31.5 %convert_add_fusion = (f32[12,512,512]{1,2,0:T(8,128)}, bf16[12,512,512]{1,2,0:T(8,128)(2,1)}, bf16[12,512,512]{1,2,0:T(8,128)(2,1)}) fusion(bf16[12,512,512]{1,2,0:T(8,128)(2,1)} %copy-done.3, bf16[12,512,512]{1,2,0:T(8,128)(2,1)} %copy-done.2, f32[12,512,512]{1,2,0:T(8,128)} %get-tuple-element.441, f32[12,512]{1,0:T(8,128)S(1)} %get-tuple-element.440, ...), kind=kLoop, calls=%fused_computation.8 | loop fusion | flops 47185920 | bytes 88178688 | tf_op jit(solution)/shard_map/while/body/eval_jaxpr/add | solution.py:125
  884.5 21.0 %reduce-scatter.47.cloned.1.call-done = bf16[768,768]{1,0:T(8,128)(2,1)} async-done(((bf16[768,3072]{1,0:T(8,128)(2,1)}), bf16[768,768]{1,0:T(8,128)(2,1)}) %reduce-scatter.47.cloned.1.call-update) | async-done | bytes 1179664 | tf_op jit(solution)/shard_map/reduce_scatter | solution.py:47
  908.4 47.5 %reduce-scatter.51.cloned.1.call-done = bf16[3072,192]{0,1:T(8,128)(2,1)} async-done(((bf16[3072,768]{0,1:T(8,128)(2,1)}), bf16[3072,192]{0,1:T(8,128)(2,1)}) %reduce-scatter.51.cloned.1.call-update) | async-done | bytes 1179664 | tf_op jit(solution)/shard_map/reduce_scatter | solution.py:50
  959.1 47.1 %reduce-scatter.35.cloned.1.call-done = bf16[768,768]{1,0:T(8,128)(2,1)} async-done(((bf16[768,3072]{1,0:T(8,128)(2,1)}), bf16[768,768]{1,0:T(8,128)(2,1)}) %reduce-scatter.35.cloned.1.call-update) | async-done | bytes 1179664 | tf_op jit(solution)/shard_map/reduce_scatter | solution.py:47
  1009.1 47.5 %reduce-scatter.39.cloned.1.call-done = bf16[3072,192]{0,1:T(8,128)(2,1)} async-done(((bf16[3072,768]{0,1:T(8,128)(2,1)}), bf16[3072,192]{0,1:T(8,128)(2,1)}) %reduce-scatter.39.cloned.1.call-update) | async-done | bytes 1179664 | tf_op jit(solution)/shard_map/reduce_scatter | solution.py:50
  1106.0 46.8 %reshape.543 = f32[12,523264]{1,0:T(8,128)} reshape(f32[12,512,1022]{2,1,0:T(8,128)} %concatenate.65.clone) | data formatting | bytes 50233344 | tf_op jit(solution)/shard_map/reshape | solution.py:78
  1152.8 90.0 %dynamic-update-slice.1 = f32[12,523776]{1,0:T(8,128)} dynamic-update-slice(f32[12,523776]{1,0:T(8,128)} %dynamic-update-slice, f32[12,523264]{1,0:T(8,128)} %reshape.543, s32[]{} %constant.330, s32[]{} %constant.331) | dynamic-update-slice | bytes 50233348
  1244.2 41.5 %reshape.544 = f32[12,512,1023]{2,1,0:T(8,128)} reshape(f32[12,523776]{1,0:T(8,128)} %dynamic-update-slice.2) | data formatting | bytes 50282496 | tf_op jit(solution)/shard_map/reshape | solution.py:83
  1295.2 39.6 %psum.7 = f32[32,12]{0,1:T(8,128)} all-reduce(f32[32,12]{0,1:T(8,128)S(1)} %fusion.105), channel_id=1, replica_groups=mesh['dp'=8,'rep'=4] {'dp','rep'}, use_global_device_ids=true, to_apply=%region_29.30 | all-reduce | flops 384 | bytes 3072 | tf_op jit(solution)/shard_map/psum | solution.py:380
  1337.7 48.1 %reduce-scatter.43.cloned.1.call-done = f32[96,576]{1,0:T(8,128)} async-done(((f32[768,576]{1,0:T(8,128)}), f32[96,576]{1,0:T(8,128)}) %reduce-scatter.43.cloned.1.call-update) | async-done | bytes 221200 | tf_op jit(solution)/shard_map/reduce_scatter | solution.py:58
  1385.8 70.1 %reduce-scatter.55.cloned.1.call-done = f32[96,576]{1,0:T(8,128)} async-done(((f32[768,576]{1,0:T(8,128)}), f32[96,576]{1,0:T(8,128)}) %reduce-scatter.55.cloned.1.call-update) | async-done | bytes 221200
  1455.9 72.1 %reduce-scatter.49.cloned.1.call-done = f32[96,768]{1,0:T(8,128)} async-done(((f32[768,768]{1,0:T(8,128)}), f32[96,768]{1,0:T(8,128)}) %reduce-scatter.49.cloned.1.call-update) | async-done | bytes 294928 | tf_op jit(solution)/shard_map/reduce_scatter | solution.py:60
  1528.0 72.1 %reduce-scatter.53.cloned.1.call-done = f32[384,192]{0,1:T(8,128)} async-done(((f32[3072,192]{0,1:T(8,128)}), f32[384,192]{0,1:T(8,128)}) %reduce-scatter.53.cloned.1.call-update) | async-done | bytes 294928 | tf_op jit(solution)/shard_map/reduce_scatter | solution.py:61
  1600.1 72.1 %reduce-scatter.37.cloned.1.call-done = f32[96,768]{1,0:T(8,128)} async-done(((f32[768,768]{1,0:T(8,128)}), f32[96,768]{1,0:T(8,128)}) %reduce-scatter.37.cloned.1.call-update) | async-done | bytes 294928 | tf_op jit(solution)/shard_map/reduce_scatter | solution.py:60
  1672.1 72.1 %reduce-scatter.41.cloned.1.call-done = f32[384,192]{0,1:T(8,128)} async-done(((f32[3072,192]{0,1:T(8,128)}), f32[384,192]{0,1:T(8,128)}) %reduce-scatter.41.cloned.1.call-update) | async-done | bytes 294928 | tf_op jit(solution)/shard_map/reduce_scatter | solution.py:61
  (596 shorter events, 595.3 us)
Async XLA Ops:
  7.2 302.3 %all-gather.15.cloned.1.call-start = ((), (), s32[]{:S(2)}) async-start(), calls=%async_computation.18 | async-start | bytes 3981312 | tf_op jit(solution)/shard_map/all_gather | solution.py:31
  17.5 336.5 %all-gather.17.cloned.1.call-start = ((), (), s32[]{:S(2)}) async-start(), calls=%async_computation.19 | async-start | bytes 1327104 | tf_op jit(solution)/shard_map/all_gather | solution.py:32
  24.9 333.5 %all-gather.19.cloned.1.call-start = ((), (), s32[]{:S(2)}) async-start(), calls=%async_computation.20 | async-start | bytes 5308416 | tf_op jit(solution)/shard_map/all_gather | solution.py:33
  33.1 363.8 %all-gather.21.cloned.1.call-start = ((), (), s32[]{:S(2)}) async-start(), calls=%async_computation.21 | async-start | bytes 5308416 | tf_op jit(solution)/shard_map/all_gather | solution.py:34
  41.3 368.4 %all-gather.23.cloned.1.call-start = ((), (), s32[]{:S(2)}) async-start(), calls=%async_computation.22 | async-start | bytes 3981312 | tf_op jit(solution)/shard_map/all_gather | solution.py:31
  50.1 406.6 %all-gather.25.cloned.1.call-start = ((), (), s32[]{:S(2)}) async-start(), calls=%async_computation.23 | async-start | bytes 1327104 | tf_op jit(solution)/shard_map/all_gather | solution.py:32
  56.7 419.8 %all-gather.27.cloned.1.call-start = ((), (), s32[]{:S(2)}) async-start(), calls=%async_computation.24 | async-start | bytes 5308416 | tf_op jit(solution)/shard_map/all_gather | solution.py:33
  64.9 492.8 %all-gather.29.cloned.1.call-start = ((), (), s32[]{:S(2)}) async-start(), calls=%async_computation.25 | async-start | bytes 5308416 | tf_op jit(solution)/shard_map/all_gather | solution.py:34
  73.1 801.4 %reduce-scatter.45.cloned.1.call-start = ((), (), s32[]{:S(2)}) async-start(), calls=%async_computation.33 | async-start | bytes 1474560 | tf_op jit(solution)/shard_map/reduce_scatter | solution.py:44
  650.0 226.7 %reduce-scatter.33.cloned.1.call-start = ((), (), s32[]{:S(2)}) async-start(), calls=%async_computation.27 | async-start | bytes 1474560 | tf_op jit(solution)/shard_map/reduce_scatter | solution.py:44
  735.6 143.3 %reduce-scatter.61.cloned.1.call-start = ((), (), s32[]{:S(2)}) async-start(), calls=%async_computation.41 | async-start | bytes 4423680
  826.7 129.2 %reduce-scatter.51.cloned.1.call-start = ((), (), s32[]{:S(2)}) async-start(), calls=%async_computation.36 | async-start | bytes 5898240 | tf_op jit(solution)/shard_map/reduce_scatter | solution.py:50
  835.8 170.3 %reduce-scatter.35.cloned.1.call-start = ((), (), s32[]{:S(2)}) async-start(), calls=%async_computation.28 | async-start | bytes 5898240 | tf_op jit(solution)/shard_map/reduce_scatter | solution.py:47
  846.4 210.2 %reduce-scatter.39.cloned.1.call-start = ((), (), s32[]{:S(2)}) async-start(), calls=%async_computation.30 | async-start | bytes 5898240 | tf_op jit(solution)/shard_map/reduce_scatter | solution.py:50
  857.4 477.4 %reduce-scatter.65.cloned.1.call-start = ((), (), s32[]{:S(2)}) async-start(), calls=%async_computation.43 | async-start | bytes 442368
  873.4 462.8 %reduce-scatter.59.cloned.1.call-start = ((), (), s32[]{:S(2)}) async-start(), calls=%async_computation.40 | async-start | bytes 442368
  874.5 463.2 %reduce-scatter.63.cloned.1.call-start = ((), (), s32[]{:S(2)}) async-start(), calls=%async_computation.42 | async-start | bytes 884736
  876.6 461.1 %reduce-scatter.57.cloned.1.call-start = ((), (), s32[]{:S(2)}) async-start(), calls=%async_computation.39 | async-start | bytes 884736
  878.8 507.0 %reduce-scatter.43.cloned.1.call-start = ((), (), s32[]{:S(2)}) async-start(), calls=%async_computation.32 | async-start | bytes 2211840 | tf_op jit(solution)/shard_map/reduce_scatter | solution.py:58
  881.8 574.0 %reduce-scatter.55.cloned.1.call-start = ((), (), s32[]{:S(2)}) async-start(), calls=%async_computation.38 | async-start | bytes 2211840
  884.5 643.6 %reduce-scatter.49.cloned.1.call-start = ((), (), s32[]{:S(2)}) async-start(), calls=%async_computation.35 | async-start | bytes 2654208 | tf_op jit(solution)/shard_map/reduce_scatter | solution.py:60
  908.3 691.7 %reduce-scatter.53.cloned.1.call-start = ((), (), s32[]{:S(2)}) async-start(), calls=%async_computation.37 | async-start | bytes 2654208 | tf_op jit(solution)/shard_map/reduce_scatter | solution.py:61
  959.0 713.1 %reduce-scatter.37.cloned.1.call-start = ((), (), s32[]{:S(2)}) async-start(), calls=%async_computation.29 | async-start | bytes 2654208 | tf_op jit(solution)/shard_map/reduce_scatter | solution.py:60
  1009.0 735.2 %reduce-scatter.41.cloned.1.call-start = ((), (), s32[]{:S(2)}) async-start(), calls=%async_computation.31 | async-start | bytes 2654208 | tf_op jit(solution)/shard_map/reduce_scatter | solution.py:61
  (163 other events, 4234.3 us)
Sparse Core Ops, SparseCore 0:
  17.7 66.0 all-gather.14
  86.5 39.4 all-gather.16
  128.2 78.6 all-gather.18
  208.8 79.1 all-gather.20
  290.0 63.3 all-gather.22
  356.1 39.5 all-gather.24
  397.8 78.6 all-gather.26
  478.6 79.1 all-gather.28
  762.2 40.4 reduce-scatter.60
  815.9 39.2 reduce-scatter.30
  857.7 47.7 reduce-scatter.46
  908.1 47.8 reduce-scatter.50
  958.3 47.8 reduce-scatter.34
  1008.7 47.8 reduce-scatter.38
  1059.7 61.4 reduce-scatter.64
  1124.3 60.4 reduce-scatter.58
  1188.6 61.5 reduce-scatter.62
  1254.3 61.5 reduce-scatter.56
  1319.9 65.8 reduce-scatter.42
  1390.3 65.5 reduce-scatter.54
  1460.0 68.0 reduce-scatter.48
  1531.9 68.0 reduce-scatter.52
  1604.1 67.9 reduce-scatter.36
  1676.1 68.1 reduce-scatter.40
  (2 shorter events, 47.7 us)
where the time goes:
time: 1760 us; the launch traced here: 1750 us
  waiting for transfers between devices  629 us (36%)
  local copies, waits for them, and re-layouts  437 us (25%)
  matrix products  392 us (22%)
  blocking collectives  182 us (10%)
  other arithmetic  92.9 us (5%)
    unnamed x350, local copies, waits for them, and re-layouts  171 us
    reduce_scatter x2, waiting for transfers between devices, push_gradients(): lax.psum_scatter(partial_set[3], 'dp', scatter_dimension=0, tiled=True)  144 us
    reduce_scatter x2, waiting for transfers between devices, push_gradients(): lax.psum_scatter(partial_set[2], 'dp', scatter_dimension=0, tiled=True)  144 us
    reduce_scatter x2, waiting for transfers between devices, push_gradients(): lax.psum_scatter(gradients[3].astype(jnp.bfloat16), 'rep', scatter_dimens...  95 us
    dot_general x2, matrix products, forward_layer(): jnp.dot(normed_low, expand, preferred_element_type=jnp.float32)  76.6 us
    unnamed x32, waiting for transfers between devices  70.5 us
    reduce_scatter x2, waiting for transfers between devices, push_gradients(): lax.psum_scatter(gradients[2].astype(jnp.bfloat16), 'rep', scatter_dimens...  68.1 us
    all_gather x2, blocking collectives, fetch_weights(): lax.all_gather(partial_set[4], 'dp', axis=1, tiled=True)  61.5 us
  transfers between devices with their start and end apart: 26, of which 12 were waited for; matrix products, arithmetic and copies ran while one was open for 47% of the time, Pallas kernels for 0%

commit v1 on v0

v1 whole, which is shorter than its diff:
```python
import functools
import jax
import jax.numpy as jnp
from jax import lax
from jax.experimental import pallas as pl
from jax.experimental.pallas import tpu as pltpu
from jax.sharding import PartitionSpec as P

F32 = jnp.float32
BF = jnp.bfloat16
LOG2E = 1.4426950408889634
NEG = -1e30
FLOOR = -1e29
VM = 60 * 1024 * 1024
NT = (((1,), (1,)), ((), ()))
TN = (((0,), (0,)), ((), ()))


def nt(a, b):
    return lax.dot_general(a, b, NT, preferred_element_type=F32)


def tn(a, b):
    return lax.dot_general(a, b, TN, preferred_element_type=F32)


def nn(a, b):
    return jnp.dot(a, b, preferred_element_type=F32)


def whole(shape):
    return pl.BlockSpec(shape, lambda *_: (0,) * len(shape))


def params():
    return pltpu.CompilerParams(vmem_limit_bytes=VM)


def prep_kernel(base, base_t, marks, bias, bias_t, mask, mask_t):
    h = pl.program_id(0)
    n = bias.shape[1]
    for src, dst in ((base, bias), (base_t, bias_t)):
        row = jnp.broadcast_to(src[0], (n, 2 * n))
        dst[0] = pltpu.roll(row, 0, 1, stride=1, stride_axis=0)[:, :n]

    @pl.when(h == 0)
    def _():
        rows = marks[...]
        seg_r, perm_r, pred_r = rows[0:1], rows[1:2], rows[2:3]
        for lo in range(0, n, 128):
            at = slice(lo, lo + 128)

            def col(k):
                piece = jnp.broadcast_to(rows[k : k + 1, at], (128, 128))
                return piece.T[:, :1]

            seg_c, perm_c, pred_c = col(0), col(1), col(2)
            same = (seg_c == seg_r) & (seg_r != 6.0)
            shown = pred_r == 0.0
            mask[0, at, :] = jnp.where(same & (shown | (perm_r <= perm_c)), 0.0, NEG)
            mask[1, at, :] = jnp.where(same & (shown | (perm_r < perm_c)), 0.0, NEG)
            same = (seg_c == seg_r) & (seg_c != 6.0)
            shown = pred_c == 0.0
            mask_t[at, :n] = jnp.where(same & (shown | (perm_c <= perm_r)), 0.0, NEG)
            mask_t[at, n:] = jnp.where(same & (shown | (perm_c < perm_r)), 0.0, NEG)


def prep(base, base_t, marks):
    heads, n2 = base.shape
    n = n2 // 2
    return pl.pallas_call(
        prep_kernel,
        grid=(heads,),
        in_specs=[
            pl.BlockSpec((1, 1, n2), lambda h: (h, 0, 0)),
            pl.BlockSpec((1, 1, n2), lambda h: (h, 0, 0)),
            whole(marks.shape),
        ],
        out_specs=[
            pl.BlockSpec((1, n, n), lambda h: (h, 0, 0)),
            pl.BlockSpec((1, n, n), lambda h: (h, 0, 0)),
            whole((2, n, n)),
            whole((n, 2 * n)),
        ],
        out_shape=[
            jax.ShapeDtypeStruct((heads, n, n), F32),
            jax.ShapeDtypeStruct((heads, n, n), F32),
            jax.ShapeDtypeStruct((2, n, n), F32),
            jax.ShapeDtypeStruct((n, 2 * n), F32),
        ],
        compiler_params=params(),
        name="prep",
    )(base.reshape(heads, 1, n2), base_t.reshape(heads, 1, n2), marks)


def bias_bases(buckets, bias_table, n):
    selector = (buckets[:, None] == jnp.arange(bias_table.shape[0], dtype=jnp.int32)[None, :]).astype(F32)
    per_offset = jnp.dot(selector, bias_table.astype(F32), precision=lax.Precision.HIGHEST).T * LOG2E
    heads = per_offset.shape[0]
    zero = jnp.zeros((heads, 1), F32)
    base = jnp.concatenate([per_offset[:, n - 1 :], zero, per_offset[:, : n - 1]], axis=1)
    flipped = per_offset[:, ::-1]
    base_t = jnp.concatenate([flipped[:, n - 1 :], zero, flipped[:, : n - 1]], axis=1)
    return selector, base, base_t


def attn_fwd_kernel(rows_at, x, y, pw, vec, bias, mask, q_o, k_o, v_o, ctx_o, lse_o, pf, lse_s):
    p = pl.program_id(0)
    n, d = x.shape
    pairs = d // 128

    @pl.when(p == 0)
    def _():
        pf[...] = jnp.concatenate([pw[r] for r in range(pw.shape[0])], axis=1)
        bq, bv = vec[0:1], vec[1:2]
        xv = x[...]
        qc = nn(xv, pf[:, :d]) + bq
        qq = nn(y[...], pf[:, :d]) + bq
        kk = nn(xv, pf[:, d : 2 * d])
        vv = nn(xv, pf[:, 2 * d :]) + bv
        for c in range(pairs):
            at = slice(128 * c, 128 * c + 128)
            q_o[c, :n] = qc[:, at].astype(BF)
            q_o[c, n:] = qq[:, at].astype(BF)
            k_o[c] = kk[:, at].astype(BF)
            v_o[c] = vv[:, at].astype(BF)
        lse_s[...] = jnp.zeros_like(lse_s)

    k = k_o[p]
    v = v_o[p]
    low = lax.broadcasted_iota(jnp.int32, (1, 128), 1) < 64
    lane = lax.broadcasted_iota(jnp.int32, (1, 128), 1)
    vx = jnp.concatenate([v, jnp.ones_like(v)], axis=1)
    k0 = jnp.where(low, k, 0)
    k1 = jnp.where(low, 0, k)
    for s in range(2):
        for lo in range(0, n, rows_at):
            at = slice(lo, lo + rows_at)
            to = slice(s * n + lo, s * n + lo + rows_at)
            q = q_o[p, to]
            outs = []
            for hh, kh in ((0, k0), (1, k1)):
                sc = nt(q, kh) * (0.125 * LOG2E) + (bias[hh, at] + mask[s, at])
                m = jnp.maximum(jnp.max(sc, axis=-1, keepdims=True), FLOOR)
                e = jnp.exp2(sc - m).astype(BF)
                r = nn(e, vx)
                tot = r[:, 128:]
                tot = jnp.where(tot > 0, tot, 1.0)
                lse = m + jnp.log2(tot)
                lse_s[to] = jnp.where(lane == 2 * p + hh, lse, lse_s[to])
                outs.append(r[:, :128] / tot)
            ctx_o[0, to] = jnp.where(low, outs[0], outs[1]).astype(BF)

    @pl.when(p == pairs - 1)
    def _():
        for lo in range(0, 2 * n, 128):
            lse_o[:, lo : lo + 128] = lse_s[lo : lo + 128].T[: lse_o.shape[0]]


def attn_fwd(x, y, pw, vec, bias, mask, rows_at=256):
    n, d = x.shape
    pairs = d // 128
    return pl.pallas_call(
        functools.partial(attn_fwd_kernel, rows_at),
        grid=(pairs,),
        in_specs=[
            whole(x.shape), whole(y.shape), whole(pw.shape), whole(vec.shape),
            pl.BlockSpec((2, n, n), lambda p: (p, 0, 0)),
            whole(mask.shape),
        ],
        out_specs=[
            whole((pairs, 2 * n, 128)), whole((pairs, n, 128)), whole((pairs, n, 128)),
            pl.BlockSpec((1, 2 * n, 128), lambda p: (p, 0, 0)),
            whole((16, 2 * n)),
        ],
        out_shape=[
            jax.ShapeDtypeStruct((pairs, 2 * n, 128), BF),
            jax.ShapeDtypeStruct((pairs, n, 128), BF),
            jax.ShapeDtypeStruct((pairs, n, 128), BF),
            jax.ShapeDtypeStruct((pairs, 2 * n, 128), BF),
            jax.ShapeDtypeStruct((16, 2 * n), F32),
        ],
        scratch_shapes=[
            pltpu.VMEM((d, 3 * d), BF),
            pltpu.VMEM((2 * n, 128), F32),
        ],
        compiler_params=params(),
        name="attn_fwd",
    )(x, y, pw, vec, bias, mask)


def gelu_parts(z):
    e = jnp.exp2(z * z * (-0.5 * LOG2E))
    den = 1.0 + (0.3275911 * 0.7071067811865476) * jnp.abs(z)
    t = pl.reciprocal(den, approx=True)
    t = t * (2.0 - den * t)
    poly = t * (0.127414796 + t * (-0.142248368 + t * (0.7107068705 + t * (-0.7265760135 + t * 0.5307027145))))
    tail = poly * e
    phi = jnp.where(z < 0, tail, 1.0 - tail)
    return z * phi, phi + z * (e * 0.3989422804014327)


def moments(v):
    centered = v - jnp.mean(v, axis=-1, keepdims=True)
    rs = lax.rsqrt(jnp.mean(centered * centered, axis=-1, keepdims=True) + 1e-05)
    return centered * rs, rs


def post_fwd_kernel(blocks, x, y, ctx, ow, ew, ct, vec, rc_o, rq_o, xh1_o, nl_o, act_o, gp_o, xh2_o, rs_o, of):
    t = pl.program_id(0)
    d = x.shape[1]
    ff = ew.shape[1]

    @pl.when(t == 0)
    def _():
        of[...] = jnp.concatenate([ow[r] for r in range(ow.shape[0])], axis=1)

    z = jnp.where(t < blocks, x[...].astype(F32), y[...].astype(F32))
    cx = jnp.concatenate([ctx[c] for c in range(ctx.shape[0])], axis=1)
    first = z + (nn(cx, of[...]) + vec[2:3])
    xh1, rs1 = moments(first)
    normed = xh1 * vec[3:4] + vec[4:5]
    nl = normed.astype(BF)
    xh1_o[...] = xh1.astype(BF)
    nl_o[...] = nl
    second = normed + vec[5:6]
    for f in range(ff // d):
        at = slice(f * d, f * d + d)
        h = nn(nl, ew[:, at]) + vec[8 + f : 9 + f]
        act, gp = gelu_parts(h)
        act = act.astype(BF)
        act_o[:, at] = act
        gp_o[:, at] = gp.astype(BF)
        second = second + nt(act, ct[:, at])
    xh2, rs2 = moments(second)
    xh2_o[...] = xh2.astype(BF)
    lane = lax.broadcasted_iota(jnp.int32, (1, 128), 1)
    rs_o[...] = jnp.where(lane < 64, rs1, rs2)
    res = (xh2 * vec[6:7] + vec[7:8]).astype(BF)

    @pl.when(t < blocks)
    def _():
        rc_o[...] = res

    @pl.when(t >= blocks)
    def _():
        rq_o[...] = res


def post_fwd(x, y, ctx, ow, ew, ct, vec, tb=256):
    n, d = x.shape
    ff = ew.shape[1]
    pairs = ctx.shape[0]
    blocks = n // tb
    first = lambda t: (jnp.minimum(t, blocks - 1), 0)
    later = lambda t: (jnp.maximum(t - blocks, 0), 0)
    row = lambda t: (t, 0)
    return pl.pallas_call(
        functools.partial(post_fwd_kernel, blocks),
        grid=(2 * blocks,),
        in_specs=[
            pl.BlockSpec((tb, d), first), pl.BlockSpec((tb, d), later),
            pl.BlockSpec((pairs, tb, 128), lambda t: (0, t, 0)),
            whole(ow.shape), whole(ew.shape), whole(ct.shape), whole(vec.shape),
        ],
        out_specs=[
            pl.BlockSpec((tb, d), first), pl.BlockSpec((tb, d), later),
            pl.BlockSpec((tb, d), row), pl.BlockSpec((tb, d), row),
            pl.BlockSpec((tb, ff), row), pl.BlockSpec((tb, ff), row),
            pl.BlockSpec((tb, d), row), pl.BlockSpec((tb, 128), row),
        ],
        out_shape=[
            jax.ShapeDtypeStruct((n, d), BF), jax.ShapeDtypeStruct((n, d), BF),
            jax.ShapeDtypeStruct((2 * n, d), BF), jax.ShapeDtypeStruct((2 * n, d), BF),
            jax.ShapeDtypeStruct((2 * n, ff), BF), jax.ShapeDtypeStruct((2 * n, ff), BF),
            jax.ShapeDtypeStruct((2 * n, d), BF), jax.ShapeDtypeStruct((2 * n, 128), F32),
        ],
        scratch_shapes=[pltpu.VMEM((d, d), BF)],
        compiler_params=params(),
        name="post_fwd",
    )(x, y, ctx, ow, ew, ct, vec)


def norm_back(g, xh, rs, gain):
    a = g * gain
    return rs * (a - jnp.mean(a, axis=-1, keepdims=True) - xh * jnp.mean(a * xh, axis=-1, keepdims=True))


def rowsum(v):
    return jnp.sum(v, axis=0, keepdims=True)


def post_bwd_kernel(blocks, gc, gq, ctx, xh1, nl, gp, xh2, rs, act, ow, ew, ct, vec,
                    first_o, gctx_o, delta_o, vg_o, do_o, de_o, dc_o,
                    of, gh_s, nl_t, gf_t, cx_t, ga_s):
    t = pl.program_id(0)
    tb, d = gc.shape
    ff = ew.shape[1]

    @pl.when(t == 0)
    def _():
        of[...] = jnp.concatenate([ow[r] for r in range(ow.shape[0])], axis=1)
        vg_o[...] = jnp.zeros_like(vg_o)

    @pl.when(t < 2 * blocks)
    def _():
        g = jnp.where(t < blocks, gc[...].astype(F32), gq[...].astype(F32))
        rs1, rs2 = rs[:, :1], rs[:, 64:65]
        xh = xh2[...].astype(F32)
        vg_o[6:7] += rowsum(g * xh)
        vg_o[7:8] += rowsum(g)
        gs = norm_back(g, xh, rs2, vec[6:7])
        gf = gs.astype(BF)
        vg_o[5:6] += rowsum(gf.astype(F32))
        gn = gs
        spot = pl.ds(pl.multiple_of(t * tb, tb), tb)
        for f in range(ff // d):
            at = slice(f * d, f * d + d)
            gh = (nn(gf, ct[:, at]) * gp[:, at].astype(F32)).astype(BF)
            gh_s[spot, at] = gh
            vg_o[8 + f : 9 + f] += rowsum(gh.astype(F32))
            gn = gn + nt(gh, ew[:, at])
        xh = xh1[...].astype(F32)
        vg_o[3:4] += rowsum(gn * xh)
        vg_o[4:5] += rowsum(gn)
        first = norm_back(gn, xh, rs1, vec[3:4])
        first_o[...] = first
        ga = first.astype(BF)
        vg_o[2:3] += rowsum(ga.astype(F32))
        ga_s[spot] = ga
        gx = nt(ga, of[...]).astype(BF)
        cx = jnp.concatenate([ctx[c] for c in range(ctx.shape[0])], axis=1)
        for c in range(ctx.shape[0]):
            gctx_o[c] = gx[:, 128 * c : 128 * c + 128]
        prod = gx.astype(F32) * cx.astype(F32)
        high = prod.astype(BF)
        rest = (prod - high.astype(F32)).astype(BF)
        heads = lax.broadcasted_iota(jnp.int32, (16, d), 0)
        spots = lax.broadcasted_iota(jnp.int32, (16, d), 1)
        pick = jnp.where((spots >= heads * 64) & (spots < heads * 64 + 64), 1.0, 0.0).astype(BF)
        delta_o[...] = nt(pick, high) + nt(pick, rest)
        nl_t[:, spot] = nl[...].T
        gf_t[:, spot] = gf.T
        cx_t[:, spot] = cx.T

    @pl.when(t == 2 * blocks)
    def _():
        do = nn(cx_t[...], ga_s[...])
        w = do_o.shape[2]
        for r in range(do_o.shape[0]):
            do_o[r] = do[:, r * w : r * w + w].astype(BF)

    for f in range(ff // d):
        @pl.when(t == 2 * blocks + f)
        def _():
            de_o[...] = nn(nl_t[...], gh_s[:, f * d : f * d + d]).astype(BF)
            dc_o[...] = nn(gf_t[...], act[...]).astype(BF)


def post_bwd(gc, gq, ctx, xh1, nl, gp, xh2, rs, act, ow, ew, ct, vec, tb=256):
    n, d = gc.shape
    ff = ew.shape[1]
    pairs = ctx.shape[0]
    blocks = n // tb
    last = 2 * blocks - 1
    tok = lambda t: (jnp.minimum(t, last), 0)
    tok3 = lambda t: (0, jnp.minimum(t, last), 0)
    col = lambda t: (0, jnp.maximum(t - last - 1, 0))
    return pl.pallas_call(
        functools.partial(post_bwd_kernel, blocks),
        grid=(2 * blocks + ff // d,),
        in_specs=[
            pl.BlockSpec((tb, d), lambda t: (jnp.minimum(t, blocks - 1), 0)),
            pl.BlockSpec((tb, d), lambda t: (jnp.clip(t - blocks, 0, blocks - 1), 0)),
            pl.BlockSpec((pairs, tb, 128), tok3),
            pl.BlockSpec((tb, d), tok), pl.BlockSpec((tb, d), tok), pl.BlockSpec((tb, ff), tok),
            pl.BlockSpec((tb, d), tok), pl.BlockSpec((tb, 128), tok),
            pl.BlockSpec((2 * n, d), col),
            whole(ow.shape), whole(ew.shape), whole(ct.shape), whole(vec.shape),
        ],
        out_specs=[
            pl.BlockSpec((tb, d), tok), pl.BlockSpec((pairs, tb, 128), tok3),
            pl.BlockSpec((16, tb), lambda t: (0, jnp.minimum(t, last))),
            whole((16, d)), whole(ow.shape),
            pl.BlockSpec((d, d), col), pl.BlockSpec((d, d), col),
        ],
        out_shape=[
            jax.ShapeDtypeStruct((2 * n, d), F32),
            jax.ShapeDtypeStruct((pairs, 2 * n, 128), BF),
            jax.ShapeDtypeStruct((16, 2 * n), F32),
            jax.ShapeDtypeStruct((16, d), F32),
            jax.ShapeDtypeStruct(ow.shape, BF),
            jax.ShapeDtypeStruct((d, ff), BF),
            jax.ShapeDtypeStruct((d, ff), BF),
        ],
        scratch_shapes=[
            pltpu.VMEM((d, d), BF), pltpu.VMEM((2 * n, ff), BF),
            pltpu.VMEM((d, 2 * n), BF), pltpu.VMEM((d, 2 * n), BF), pltpu.VMEM((d, 2 * n), BF),
            pltpu.VMEM((2 * n, d), BF),
        ],
        compiler_params=params(),
        name="post_bwd",
    )(gc, gq, ctx, xh1, nl, gp, xh2, rs, act, ow, ew, ct, vec)


def attn_bwd_kernel(rows_at, q, k, v, go, lse, delta, bias_t, mask_t, x, y, first, pw,
                    gx_o, gy_o, dp_o, bg_o, t8_o, pf, dq_s, dk_s, dv_s, diag, x_t):
    p = pl.program_id(0)
    n, d = x.shape
    pairs = d // 128
    wide = diag.shape[2]

    @pl.when(p == 0)
    def _():
        pf[...] = jnp.concatenate([pw[r] for r in range(pw.shape[0])], axis=1)
        x_t[:, :n] = x[...].T
        x_t[:, n:] = y[...].T

    @pl.when(p < pairs)
    def _():
        low = lax.broadcasted_iota(jnp.int32, (1, 128), 1) < 64
        qa, ga = q[0], go[0]
        qm = (jnp.where(low, qa, 0), jnp.where(low, 0, qa))
        gm = (jnp.where(low, ga, 0), jnp.where(low, 0, ga))
        dq = jnp.zeros((2 * n, 128), F32)
        diag[...] = jnp.zeros_like(diag)
        for lo in range(0, n, rows_at):
            at = slice(lo, lo + rows_at)
            ka, va = k[0, at], v[0, at]
            dk = jnp.zeros((rows_at, 128), F32)
            dv = jnp.zeros((rows_at, 128), F32)
            for hh in range(2):
                km = jnp.where(low, ka, 0) if hh == 0 else jnp.where(low, 0, ka)
                vm = jnp.where(low, va, 0) if hh == 0 else jnp.where(low, 0, va)
                lrow = lse[pl.ds(2 * p + hh, 1)]
                drow = delta[pl.ds(2 * p + hh, 1)]
                bias = bias_t[hh, at]
                both = jnp.concatenate([bias, bias], axis=1) + mask_t[at]
                sc = nt(km, qa) * (0.125 * LOG2E) + both
                pr = jnp.exp2(sc - lrow)
                ds = pr * (nt(vm, ga) - drow)
                dsb = ds.astype(BF)
                dv = dv + nn(pr.astype(BF), gm[hh])
                dk = dk + nn(dsb, qm[hh])
                dq = dq + tn(dsb, km)
                for b in range(0, rows_at, 128):
                    off = 384 - (lo + b)
                    diag[hh, :, off : off + n] += ds[b : b + 128, :n] + ds[b : b + 128, n:]
            dk_s[p, at] = (dk * 0.125).astype(BF)
            dv_s[p, at] = dv.astype(BF)
        dq_s[p] = (dq * 0.125).astype(BF)
        for hh in range(2):
            total = jnp.zeros((8, 2 * n), F32)
            for g in range(16):
                piece = jnp.concatenate([diag[hh, 8 * g : 8 * g + 8], jnp.zeros((8, 2 * n - wide), F32)], axis=1)
                total = total + (pltpu.roll(piece, 2 * n - 8 * g, 1) if g else piece)
            t8_o[hh] = total

    @pl.when(p == pairs)
    def _():
        cat = lambda ref, at: jnp.concatenate([ref[c, at] for c in range(pairs)], axis=1)
        gqc, gqq = cat(dq_s, slice(0, n)), cat(dq_s, slice(n, 2 * n))
        gk, gv = cat(dk_s, slice(0, n)), cat(dv_s, slice(0, n))
        gx_o[...] = first[:n] + nt(gqc, pf[:, :d]) + nt(gk, pf[:, d : 2 * d]) + nt(gv, pf[:, 2 * d :])
        gy_o[...] = first[n:] + nt(gqq, pf[:, :d])
        bg_o[...] = jnp.zeros_like(bg_o)
        bg_o[0:1] = rowsum(gqc.astype(F32)) + rowsum(gqq.astype(F32))
        bg_o[1:2] = rowsum(gv.astype(F32))
        xt = x_t[:, :n]
        grads = jnp.concatenate([
            nn(x_t[...], jnp.concatenate([gqc, gqq], axis=0)).astype(BF),
            nn(xt, gk).astype(BF), nn(xt, gv).astype(BF)], axis=1)
        w = dp_o.shape[2]
        for r in range(dp_o.shape[0]):
            dp_o[r] = grads[:, r * w : r * w + w]


def attn_bwd(q, k, v, go, lse, delta, bias_t, mask_t, x, y, first, pw, rows_at=256):
    n, d = x.shape
    pairs = d // 128
    pair = lambda p: (jnp.minimum(p, pairs - 1), 0, 0)
    return pl.pallas_call(
        functools.partial(attn_bwd_kernel, rows_at),
        grid=(pairs + 1,),
        in_specs=[
            pl.BlockSpec((1, 2 * n, 128), pair), pl.BlockSpec((1, n, 128), pair),
            pl.BlockSpec((1, n, 128), pair), pl.BlockSpec((1, 2 * n, 128), pair),
            whole(lse.shape), whole(delta.shape),
            pl.BlockSpec((2, n, n), pair), whole(mask_t.shape),
            whole(x.shape), whole(y.shape), whole(first.shape), whole(pw.shape),
        ],
        out_specs=[
            whole((n, d)), whole((n, d)), whole(pw.shape), whole((8, d)),
            pl.BlockSpec((2, 8, 2 * n), pair),
        ],
        out_shape=[
            jax.ShapeDtypeStruct((n, d), F32), jax.ShapeDtypeStruct((n, d), F32),
            jax.ShapeDtypeStruct(pw.shape, BF), jax.ShapeDtypeStruct((8, d), F32),
            jax.ShapeDtypeStruct((2 * pairs, 8, 2 * n), F32),
        ],
        scratch_shapes=[
            pltpu.VMEM((d, 3 * d), BF), pltpu.VMEM((pairs, 2 * n, 128), BF),
            pltpu.VMEM((pairs, n, 128), BF), pltpu.VMEM((pairs, n, 128), BF),
            pltpu.VMEM((2, 128, n + 384), F32), pltpu.VMEM((d, 2 * n), BF),
        ],
        compiler_params=params(),
        name="attn_bwd",
    )(q, k, v, go, lse, delta, bias_t, mask_t, x, y, first, pw)


def offset_sums(t8):
    heads, eight, n2 = t8.shape
    n = n2 // 2
    total = sum(jnp.roll(t8[:, r], -(384 + r), axis=1) for r in range(eight))
    return jnp.concatenate([total[:, 1:n][:, ::-1], total[:, :1], total[:, n + 1 :][:, ::-1]], axis=1)


def gather_layer(project, output, expand, contract, vectors):
    rows = lambda a, dim: lax.all_gather(a, "dp", axis=dim, tiled=True)
    pw = lax.all_gather(rows(project, 0), "rep", axis=0)
    ow = lax.all_gather(rows(output, 0), "rep", axis=0)
    ew = lax.all_gather(rows(expand, 0), "rep", axis=1, tiled=True)
    ct = lax.all_gather(rows(contract.T, 1), "rep", axis=0, tiled=True)
    vec = lax.all_gather(rows(vectors, 1), "rep", axis=0, tiled=True).astype(F32)
    return pw, ow, ew, ct, vec


def scatter_sum(a, rep_dim, dp_dim):
    a = lax.psum_scatter(a, "rep", scatter_dimension=rep_dim, tiled=True)
    return lax.psum_scatter(a, "dp", scatter_dimension=dp_dim, tiled=True).astype(F32)


def scatter_layer(dp, do, de, dc, vec):
    return (
        scatter_sum(dp, 0, 1)[0],
        scatter_sum(do, 0, 1)[0],
        scatter_sum(de, 1, 0),
        scatter_sum(dc, 0, 1).T,
        scatter_sum(vec, 0, 1),
    )


def shards(
    content_stream, query_stream, segments, perm_order, predicted, buckets, bias_table,
    project_one, output_one, expand_one, contract_one, vectors_one,
    project_two, output_two, expand_two, contract_two, vectors_two,
    content_cotangent, query_cotangent,
):
    shape = content_stream.shape
    n, d = shape[1:]
    flat = lambda a: a.reshape(n, d)
    selector, base, base_t = bias_bases(buckets, bias_table, n)
    marks = jnp.concatenate([segments, perm_order, predicted, jnp.zeros((5, n), jnp.int32)]).astype(F32)
    bias, bias_t, mask, mask_t = prep(base, base_t, marks)
    layers = (
        gather_layer(project_one, output_one, expand_one, contract_one, vectors_one),
        gather_layer(project_two, output_two, expand_two, contract_two, vectors_two),
    )
    x, y = flat(content_stream), flat(query_stream)
    kept = []
    for pw, ow, ew, ct, vec in layers:
        q, k, v, ctx, lse = attn_fwd(x, y, pw, vec, bias, mask)
        nx, ny, xh1, nl, act, gp, xh2, rs = post_fwd(x, y, ctx, ow, ew, ct, vec)
        kept.append((x, y, q, k, v, ctx, lse, xh1, nl, act, gp, xh2, rs))
        x, y = nx, ny
    gx, gy = flat(content_cotangent), flat(query_cotangent)
    grads, sums = [], []
    for (pw, ow, ew, ct, vec), saved in zip(layers[::-1], kept[::-1]):
        ix, iy, q, k, v, ctx, lse, xh1, nl, act, gp, xh2, rs = saved
        first, gctx, delta, vg, do, de, dc = post_bwd(gx, gy, ctx, xh1, nl, gp, xh2, rs, act, ow, ew, ct, vec)
        gx, gy, dp, bg, t8 = attn_bwd(q, k, v, gctx, lse, delta, bias_t, mask_t, ix, iy, first, pw)
        vg = jnp.concatenate([bg[:2], vg[2:12]], axis=0)
        grads.append(scatter_layer(dp, do, de, dc, vg))
        sums.append(t8)
    distances = offset_sums(sums[0] + sums[1])
    table = jnp.dot(selector.T, distances.T, precision=lax.Precision.HIGHEST)
    table = lax.psum(table, ("dp", "rep"))
    return (
        x.reshape(shape), y.reshape(shape), gx.reshape(shape), gy.reshape(shape), table,
        *grads[1], *grads[0],
    )


def solution(mesh):
    rows3, rows2 = P(("dp", "rep"), None, None), P(("dp", "rep"), None)
    weights = (P("dp", "rep"),) * 4 + (P("rep", "dp"),)
    return jax.shard_map(
        shards,
        mesh=mesh,
        in_specs=(rows3, rows3, rows2, rows2, rows2, P(), P(), *weights, *weights, rows3, rows3),
        out_specs=(rows3, rows3, rows3, rows3, P(), *weights, *weights),
        check_vma=False,
    )
```

time: 1760 us -> 1700 us (0.966)
  waiting for transfers between devices: 629 us -> 1150 us
  local copies, waits for them, and re-layouts: 437 us -> 21.1 us
  matrix products: 392 us -> 0.74 us
  Pallas kernels: 0 us -> 267 us
  other arithmetic: 92.9 us -> 13.2 us
  blocking collectives: 182 us -> 225 us
    dot_general x52 -> x2, matrix products: 346 us -> 0.74 us  [the longest x1 0.42 us: shards(): table = jnp.dot(selector.T, distances.T, precision=lax.Precision.HIGHEST)]
    pallas_call x0 -> x9, Pallas kernels: none -> 267 us  [the longest x2 78 us: post_bwd(): pl.pallas_call(functools.partial(post_bwd_kernel, blocks), grid=(2 * bloc...]
    reduce_scatter x12 -> x14, waiting for transfers between devices: 500 us -> 728 us  [the longest x6 383 us: scatter_sum(): lax.psum_scatter(a, 'dp', scatter_dimension=dp_dim, tiled=True).astype(F32)]
    unnamed x32 -> x36, waiting for transfers between devices: 70.5 us -> 253 us
    unnamed x350 -> x47, local copies, waits for them, and re-layouts: 171 us -> 15 us
    reshape x12 -> x2, local copies, waits for them, and re-layouts: 144 us -> 1.33 us  [the longest x1 0.67 us: prep(): base.reshape(heads, 1, n2)]
    all_gather x8 -> x12, waiting for transfers between devices: 58.6 us -> 169 us  [the longest x2 78 us: gather_layer(): ct = lax.all_gather(rows(contract.T, 1), 'rep', axis=0, tiled=True)]
    all_gather x12 -> x8, blocking collectives: 131 us -> 186 us  [the longest x6 175 us: gather_layer(): rows = lambda a, dim: lax.all_gather(a, 'dp', axis=dim, tiled=True)]
  transfers between devices with their start and end apart: 26 -> 31, of which waited for: 12 -> 27; matrix products, arithmetic and copies ran while one was open for 47% -> 2% of each run, Pallas kernels for 0% -> 5%
where the time goes in v1:
time: 1700 us; the launch traced here: 1690 us
  waiting for transfers between devices  1150 us (68%)
  Pallas kernels  267 us (16%)
  blocking collectives  225 us (13%)
  local copies, waits for them, and re-layouts  21.1 us (1%)
    reduce_scatter x6, waiting for transfers between devices, scatter_sum(): lax.psum_scatter(a, 'dp', scatter_dimension=dp_dim, tiled=True).astype(F32)  383 us
    reduce_scatter x8, waiting for transfers between devices, scatter_sum(): a = lax.psum_scatter(a, 'rep', scatter_dimension=rep_dim, tiled=True)  345 us
    unnamed x36, waiting for transfers between devices  253 us
    all_gather x6, blocking collectives, gather_layer(): rows = lambda a, dim: lax.all_gather(a, 'dp', axis=dim, tiled=True)  175 us
    all_gather x2, waiting for transfers between devices, gather_layer(): ct = lax.all_gather(rows(contract.T, 1), 'rep', axis=0, tiled=True)  78 us
    pallas_call x2, Pallas kernels, post_bwd(): pl.pallas_call(functools.partial(post_bwd_kernel, blocks), grid=(2 * bloc...  78 us
    pallas_call x2, Pallas kernels, attn_bwd(): pl.pallas_call(functools.partial(attn_bwd_kernel, rows_at), grid=(pairs +...  73.4 us
    pallas_call x2, Pallas kernels, post_fwd(): pl.pallas_call(functools.partial(post_fwd_kernel, blocks), grid=(2 * bloc...  61.4 us
  transfers between devices with their start and end apart: 31, of which 27 were waited for; matrix products, arithmetic and copies ran while one was open for 2% of the time, Pallas kernels for 5%

profile of v1, /device:TPU:0, one launch (start us, length us, event | category | flops | bytes accessed | tf_op | source)
XLA Modules:
  0.0 1693.6 jit_solution(4699667237320719573)
XLA Ops:
  10.0 37.4 %all_gather.72 = bf16[768,576]{1,0:T(8,128)(2,1)} all-gather(bf16[96,576]{1,0:T(8,128)(2,1)} %param.26), channel_id=1, replica_groups=mesh['dp'=8,'rep'=4] {'dp'}, dimensions={0}, use_global_device_ids=true | all-gather | bytes 995328 | tf_op jit(solution)/shard_map/all_gather | solution.py:519
  283.8 39.1 %all-gather.27.cloned.1.call-done.ct = bf16[768,3072]{1,0:T(8,128)(2,1)} async-done(((bf16[192,3072]{1,0:T(8,128)(2,1)}), bf16[768,3072]{1,0:T(8,128)(2,1)}) %all-gather.27.cloned.1.call-update) | async-done | bytes 4718608 | tf_op jit(solution)/shard_map/all_gather | solution.py:523
  378.6 39.1 %all-gather.31.cloned.1.call-done.ew = bf16[768,3072]{1,0:T(8,128)(2,1)} async-done(((bf16[768,768]{1,0:T(8,128)(2,1)}), bf16[768,3072]{1,0:T(8,128)(2,1)}) %all-gather.31.cloned.1.call-update) | async-done | bytes 4718608 | tf_op jit(solution)/shard_map/all_gather | solution.py:522
  417.6 38.9 %all-gather.35.cloned.1.call-done.ct = bf16[768,3072]{1,0:T(8,128)(2,1)} async-done(((bf16[192,3072]{1,0:T(8,128)(2,1)}), bf16[768,3072]{1,0:T(8,128)(2,1)}) %all-gather.35.cloned.1.call-update) | async-done | bytes 4718608 | tf_op jit(solution)/shard_map/all_gather | solution.py:523
  487.2 39.1 %post_bwd.2 = (f32[1024,768]{1,0:T(8,128)}, bf16[6,1024,128]{2,1,0:T(8,128)(2,1)}, f32[16,1024]{1,0:T(8,128)}, f32[16,768]{1,0:T(8,128)}, bf16[4,768,192]{2,1,0:...) custom-call(bf16[512,768]{1,0:T(8,128)(2,1)} %bitcast.98, bf16[512,768]{1,0:T(8,128)(2,1)} %bitcast.99, ...), custom_call_target="tpu_custom_call" | custom-call | tf_op jit(solution)/shard_map/post_bwd/pallas_call | solution.py:369
  526.3 36.7 %attn_bwd.2 = (f32[512,768]{1,0:T(8,128)}, f32[512,768]{1,0:T(8,128)}, bf16[4,768,576]{2,1,0:T(8,128)(2,1)}, f32[8,768]{1,0:T(8,128)}, f32[12,8,1024]{2,1,0:T(8,128)}) custom-call(bf16[6,1024,128]{2,1,0:T(8,128)(2,1)} %get-tuple-element.80.q, bf16[6,512,128]{2,1,0:T(8,128)(2,1)} %get-tuple-element.81.k, bf16[6,512,128]{2,1,0:T(8,128)(2,1)} %get-tuple-element.82.v, ...), custom_call_target="tpu_custom_call" | custom-call | tf_op jit(solution)/shard_map/attn_bwd/pallas_call | solution.py:482
  563.0 38.9 %post_bwd.3 = (f32[1024,768]{1,0:T(8,128)}, bf16[6,1024,128]{2,1,0:T(8,128)(2,1)}, f32[16,1024]{1,0:T(8,128)}, f32[16,768]{1,0:T(8,128)}, bf16[4,768,192]{2,1,0:...) custom-call(f32[512,768]{1,0:T(8,128)} %get-tuple-element.95.gc, f32[512,768]{1,0:T(8,128)} %get-tuple-element.96.gq, ...), custom_call_target="tpu_custom_call" | custom-call | tf_op jit(solution)/shard_map/post_bwd/pallas_call | solution.py:369
  602.7 36.8 %attn_bwd.3 = (f32[512,768]{1,0:T(8,128)}, f32[512,768]{1,0:T(8,128)}, bf16[4,768,576]{2,1,0:T(8,128)(2,1)}, f32[8,768]{1,0:T(8,128)}, f32[12,8,1024]{2,1,0:T(8,128)}) custom-call(bf16[6,1024,128]{2,1,0:T(8,128)(2,1)} %get-tuple-element.77.q, bf16[6,512,128]{2,1,0:T(8,128)(2,1)} %get-tuple-element.78.k, bf16[6,512,128]{2,1,0:T(8,128)(2,1)} %get-tuple-element.79.v, ...), custom_call_target="tpu_custom_call" | custom-call | tf_op jit(solution)/shard_map/attn_bwd/pallas_call | solution.py:482
  735.2 45.4 %reduce-scatter.27.cloned.1.call-done = bf16[1,768,576]{2,1,0:T(8,128)(2,1)} async-done(((bf16[4,768,576]{2,1,0:T(8,128)(2,1)}), bf16[1,768,576]{2,1,0:T(8,128)(2,1)}) %reduce-scatter.27.cloned.1.call-update) | async-done | bytes 884752 | tf_op jit(solution)/shard_map/reduce_scatter | solution.py:529
  780.7 45.2 %reduce-scatter.41.cloned.1.call-done = bf16[1,768,576]{2,1,0:T(8,128)(2,1)} async-done(((bf16[4,768,576]{2,1,0:T(8,128)(2,1)}), bf16[1,768,576]{2,1,0:T(8,128)(2,1)}) %reduce-scatter.41.cloned.1.call-update) | async-done | bytes 884752 | tf_op jit(solution)/shard_map/reduce_scatter | solution.py:529
  826.0 50.4 %reduce-scatter.39.cloned.1.call-done = bf16[192,3072]{1,0:T(8,128)(2,1)} async-done(((bf16[768,3072]{1,0:T(8,128)(2,1)}), bf16[192,3072]{1,0:T(8,128)(2,1)}) %reduce-scatter.39.cloned.1.call-update) | async-done | bytes 1179664 | tf_op jit(solution)/shard_map/reduce_scatter | solution.py:529
  879.0 47.8 %reduce-scatter.53.cloned.1.call-done = bf16[192,3072]{1,0:T(8,128)(2,1)} async-done(((bf16[768,3072]{1,0:T(8,128)(2,1)}), bf16[192,3072]{1,0:T(8,128)(2,1)}) %reduce-scatter.53.cloned.1.call-update) | async-done | bytes 1179664 | tf_op jit(solution)/shard_map/reduce_scatter | solution.py:529
  929.4 47.8 %reduce-scatter.35.cloned.1.call-done = bf16[768,768]{1,0:T(8,128)(2,1)} async-done(((bf16[768,3072]{1,0:T(8,128)(2,1)}), bf16[768,768]{1,0:T(8,128)(2,1)}) %reduce-scatter.35.cloned.1.call-update) | async-done | bytes 1179664 | tf_op jit(solution)/shard_map/reduce_scatter | solution.py:529
  977.9 49.8 %reduce-scatter.49.cloned.1.call-done = bf16[768,768]{1,0:T(8,128)(2,1)} async-done(((bf16[768,3072]{1,0:T(8,128)(2,1)}), bf16[768,768]{1,0:T(8,128)(2,1)}) %reduce-scatter.49.cloned.1.call-update) | async-done | bytes 1179664 | tf_op jit(solution)/shard_map/reduce_scatter | solution.py:529
  1029.6 39.6 %psum.7 = f32[32,12]{0,1:T(8,128)} all-reduce(f32[32,12]{0,1:T(8,128)S(1)} %fusion), channel_id=1, replica_groups=mesh['dp'=8,'rep'=4] {'dp','rep'}, use_global_device_ids=true, to_apply=%region_0.0 | all-reduce | flops 384 | bytes 3072 | tf_op jit(solution)/shard_map/psum | solution.py:577
  1094.1 62.6 %reduce-scatter.61.cloned.1.call-done = f32[96,3]{1,0:T(8,128)} async-done(((f32[768,3]{1,0:T(8,128)}), f32[96,3]{1,0:T(8,128)}) %reduce-scatter.61.cloned.1.call-update) | async-done | bytes 1168
  1158.2 62.4 %reduce-scatter.33.cloned.1.call-done = bf16[1,96,192]{2,1,0:T(8,128)(2,1)} async-done(((bf16[1,768,192]{2,1,0:T(8,128)(2,1)}), bf16[1,96,192]{2,1,0:T(8,128)(2,1)}) %reduce-scatter.33.cloned.1.call-update) | async-done | bytes 36880 | tf_op jit(solution)/shard_map/reduce_scatter | solution.py:530
  1222.1 62.6 %reduce-scatter.47.cloned.1.call-done = bf16[1,96,192]{2,1,0:T(8,128)(2,1)} async-done(((bf16[1,768,192]{2,1,0:T(8,128)(2,1)}), bf16[1,96,192]{2,1,0:T(8,128)(2,1)}) %reduce-scatter.47.cloned.1.call-update) | async-done | bytes 36880 | tf_op jit(solution)/shard_map/reduce_scatter | solution.py:530
  1286.1 64.4 %reduce-scatter.29.cloned.1.call-done = bf16[1,96,576]{2,1,0:T(8,128)(2,1)} async-done(((bf16[1,768,576]{2,1,0:T(8,128)(2,1)}), bf16[1,96,576]{2,1,0:T(8,128)(2,1)}) %reduce-scatter.29.cloned.1.call-update) | async-done | bytes 110608 | tf_op jit(solution)/shard_map/reduce_scatter | solution.py:530
  1352.2 63.9 %reduce-scatter.43.cloned.1.call-done = bf16[1,96,576]{2,1,0:T(8,128)(2,1)} async-done(((bf16[1,768,576]{2,1,0:T(8,128)(2,1)}), bf16[1,96,576]{2,1,0:T(8,128)(2,1)}) %reduce-scatter.43.cloned.1.call-update) | async-done | bytes 110608 | tf_op jit(solution)/shard_map/reduce_scatter | solution.py:530
  1417.7 66.1 %reduce-scatter.55.cloned.1.call-done = bf16[384,192]{1,0:T(8,128)(2,1)} async-done(((bf16[3072,192]{1,0:T(8,128)(2,1)}), bf16[384,192]{1,0:T(8,128)(2,1)}) %reduce-scatter.55.cloned.1.call-update) | async-done | bytes 147472
  1484.9 66.2 %reduce-scatter.59.cloned.1.call-done = bf16[384,192]{1,0:T(8,128)(2,1)} async-done(((bf16[3072,192]{1,0:T(8,128)(2,1)}), bf16[384,192]{1,0:T(8,128)(2,1)}) %reduce-scatter.59.cloned.1.call-update) | async-done | bytes 147472
  1552.3 65.6 %reduce-scatter.37.cloned.1.call-done = bf16[96,768]{1,0:T(8,128)(2,1)} async-done(((bf16[768,768]{1,0:T(8,128)(2,1)}), bf16[96,768]{1,0:T(8,128)(2,1)}) %reduce-scatter.37.cloned.1.call-update) | async-done | bytes 147472 | tf_op jit(solution)/shard_map/reduce_scatter | solution.py:530
  1621.0 63.7 %reduce-scatter.51.cloned.1.call-done = bf16[96,768]{1,0:T(8,128)(2,1)} async-done(((bf16[768,768]{1,0:T(8,128)(2,1)}), bf16[96,768]{1,0:T(8,128)(2,1)}) %reduce-scatter.51.cloned.1.call-update) | async-done | bytes 147472 | tf_op jit(solution)/shard_map/reduce_scatter | solution.py:530
  (191 shorter events, 468.1 us)
Async XLA Ops:
  10.0 244.6 %all-gather.37.cloned.1.call-start = ((), (), s32[]{:S(2)}) async-start(), calls=%async_computation.40 | async-start | bytes 4915200 | tf_op jit(solution)/shard_map/all_gather | solution.py:520
  47.5 227.4 %all-gather.39.cloned.1.call-start = ((), (), s32[]{:S(2)}) async-start(), calls=%async_computation.41 | async-start | bytes 1966080 | tf_op jit(solution)/shard_map/all_gather | solution.py:521
  81.0 202.7 %all-gather.23.cloned.1.call-start = ((), (), s32[]{:S(2)}) async-start(), calls=%async_computation.19 | async-start | bytes 5898240 | tf_op jit(solution)/shard_map/all_gather | solution.py:522
  81.8 241.0 %all-gather.27.cloned.1.call-start = ((), (), s32[]{:S(2)}) async-start(), calls=%async_computation.21 | async-start | bytes 5898240 | tf_op jit(solution)/shard_map/all_gather | solution.py:523
  100.5 257.0 %all-gather.41.cloned.1.call-start = ((), (), s32[]{:S(2)}) async-start(), calls=%async_computation.42 | async-start | bytes 4915200 | tf_op jit(solution)/shard_map/all_gather | solution.py:520
  136.5 242.1 %all-gather.43.cloned.1.call-start = ((), (), s32[]{:S(2)}) async-start(), calls=%async_computation.43 | async-start | bytes 1966080 | tf_op jit(solution)/shard_map/all_gather | solution.py:521
  169.9 247.7 %all-gather.31.cloned.1.call-start = ((), (), s32[]{:S(2)}) async-start(), calls=%async_computation.23 | async-start | bytes 5898240 | tf_op jit(solution)/shard_map/all_gather | solution.py:522
  170.7 285.8 %all-gather.35.cloned.1.call-start = ((), (), s32[]{:S(2)}) async-start(), calls=%async_computation.25 | async-start | bytes 5898240 | tf_op jit(solution)/shard_map/all_gather | solution.py:523
  190.1 483.7 %all-reduce.5.cloned.1.call-start = ((), (), s32[]{:S(2)}) async-start(), calls=%async_computation.48 | async-start | bytes 196608
  644.0 182.0 %reduce-scatter.41.cloned.1.call-start = ((), (), s32[]{:S(2)}) async-start(), calls=%async_computation.33 | async-start | bytes 4915200 | tf_op jit(solution)/shard_map/reduce_scatter | solution.py:529
  644.6 231.8 %reduce-scatter.39.cloned.1.call-start = ((), (), s32[]{:S(2)}) async-start(), calls=%async_computation.32 | async-start | bytes 5898240 | tf_op jit(solution)/shard_map/reduce_scatter | solution.py:529
  645.1 281.7 %reduce-scatter.53.cloned.1.call-start = ((), (), s32[]{:S(2)}) async-start(), calls=%async_computation.39 | async-start | bytes 5898240 | tf_op jit(solution)/shard_map/reduce_scatter | solution.py:529
  645.9 331.3 %reduce-scatter.35.cloned.1.call-start = ((), (), s32[]{:S(2)}) async-start(), calls=%async_computation.30 | async-start | bytes 5898240 | tf_op jit(solution)/shard_map/reduce_scatter | solution.py:529
  646.5 381.2 %reduce-scatter.49.cloned.1.call-start = ((), (), s32[]{:S(2)}) async-start(), calls=%async_computation.37 | async-start | bytes 5898240 | tf_op jit(solution)/shard_map/reduce_scatter | solution.py:529
  647.2 445.5 %reduce-scatter.57.cloned.1.call-start = ((), (), s32[]{:S(2)}) async-start(), calls=%async_computation.45 | async-start | bytes 442368
  675.6 481.1 %reduce-scatter.61.cloned.1.call-start = ((), (), s32[]{:S(2)}) async-start(), calls=%async_computation.47 | async-start | bytes 442368
  676.6 544.0 %reduce-scatter.33.cloned.1.call-start = ((), (), s32[]{:S(2)}) async-start(), calls=%async_computation.29 | async-start | bytes 442368 | tf_op jit(solution)/shard_map/reduce_scatter | solution.py:530
  704.6 580.1 %reduce-scatter.47.cloned.1.call-start = ((), (), s32[]{:S(2)}) async-start(), calls=%async_computation.36 | async-start | bytes 442368 | tf_op jit(solution)/shard_map/reduce_scatter | solution.py:530
  735.2 615.4 %reduce-scatter.29.cloned.1.call-start = ((), (), s32[]{:S(2)}) async-start(), calls=%async_computation.27 | async-start | bytes 1105920 | tf_op jit(solution)/shard_map/reduce_scatter | solution.py:530
  780.7 635.5 %reduce-scatter.43.cloned.1.call-start = ((), (), s32[]{:S(2)}) async-start(), calls=%async_computation.34 | async-start | bytes 1105920 | tf_op jit(solution)/shard_map/reduce_scatter | solution.py:530
  826.0 657.9 %reduce-scatter.55.cloned.1.call-start = ((), (), s32[]{:S(2)}) async-start(), calls=%async_computation.44 | async-start | bytes 1769472
  878.9 672.3 %reduce-scatter.59.cloned.1.call-start = ((), (), s32[]{:S(2)}) async-start(), calls=%async_computation.46 | async-start | bytes 1769472
  929.3 688.5 %reduce-scatter.37.cloned.1.call-start = ((), (), s32[]{:S(2)}) async-start(), calls=%async_computation.31 | async-start | bytes 1327104 | tf_op jit(solution)/shard_map/reduce_scatter | solution.py:530
  977.2 707.5 %reduce-scatter.51.cloned.1.call-start = ((), (), s32[]{:S(2)}) async-start(), calls=%async_computation.38 | async-start | bytes 1327104 | tf_op jit(solution)/shard_map/reduce_scatter | solution.py:530
  (22 other events, 1978.2 us)
Sparse Core Ops, SparseCore 0:
  10.2 47.3 all-gather.20
  59.7 40.6 all-gather.24
  102.6 44.0 all-gather.28
  148.6 41.4 all-gather.32
  246.3 37.4 all-gather.22
  285.3 37.4 all-gather.26
  380.1 37.4 all-gather.30
  419.1 37.4 all-gather.34
  737.7 42.8 reduce-scatter.26
  783.0 42.8 reduce-scatter.40
  828.5 47.8 reduce-scatter.38
  878.9 47.8 reduce-scatter.52
  929.3 47.8 reduce-scatter.34
  979.8 47.8 reduce-scatter.48
  1031.2 61.3 reduce-scatter.56
  1096.3 60.3 reduce-scatter.60
  1160.2 60.3 reduce-scatter.32
  1224.2 60.3 reduce-scatter.46
  1288.2 62.2 reduce-scatter.28
  1353.8 62.3 reduce-scatter.42
  1419.9 63.8 reduce-scatter.54
  1487.3 63.8 reduce-scatter.58
  1554.8 63.0 reduce-scatter.36
  1621.7 63.0 reduce-scatter.50
  (7 shorter events, 191.8 us)

commit v2 on v1

v2 whole, which is shorter than its diff:
```python
import functools
import jax
import jax.numpy as jnp
from jax import lax
from jax.experimental import pallas as pl
from jax.experimental.pallas import tpu as pltpu
from jax.sharding import PartitionSpec as P

F32 = jnp.float32
BF = jnp.bfloat16
LOG2E = 1.4426950408889634
NEG = -1e30
FLOOR = -1e29
VM = 60 * 1024 * 1024
NT = (((1,), (1,)), ((), ()))
TN = (((0,), (0,)), ((), ()))


def nt(a, b):
    return lax.dot_general(a, b, NT, preferred_element_type=F32)


def tn(a, b):
    return lax.dot_general(a, b, TN, preferred_element_type=F32)


def nn(a, b):
    return jnp.dot(a, b, preferred_element_type=F32)


def whole(shape):
    return pl.BlockSpec(shape, lambda *_: (0,) * len(shape))


def params(number=None):
    if number is None:
        return pltpu.CompilerParams(vmem_limit_bytes=VM)
    return pltpu.CompilerParams(vmem_limit_bytes=VM, collective_id=number, has_side_effects=True)


MESH = pl.DeviceIdType.MESH
ANY = pl.BlockSpec(memory_space=pl.ANY)
SEMS = 18


class Place:
    def __init__(self):
        self.dp = lax.axis_index("dp")
        self.rep = lax.axis_index("rep")
        self.z, self.x = self.dp // 2, self.dp % 2
        self.y, self.c = self.rep // 2, self.rep % 2
        self.dx, self.dy, self.dc = 1 - 2 * self.x, 2 - 4 * self.y, 1 - 2 * self.c
        self.across_x = (self.dp + self.dx, self.rep)
        self.across_y = (self.dp, self.rep + self.dy)
        self.other_core = (self.dp, self.rep + self.dc)

    def plane(self, k):
        return ((self.z + k) % 4, self.x)

    def to_plane(self, k):
        return (((self.z + k) % 4) * 2 + self.x, self.rep)

    def from_plane(self, k):
        return ((self.z + 4 - k) % 4) * 2 + self.x

    def greet(self):
        barrier = pltpu.get_barrier_semaphore()
        peers = [self.to_plane(k) for k in (1, 2, 3)] + [self.across_x, self.across_y, self.other_core]
        for peer in peers:
            pl.semaphore_signal(barrier, inc=1, device_id=peer, device_id_type=MESH)
        pl.semaphore_wait(barrier, len(peers))


def remote(src, dst, send, recv, peer):
    return pltpu.make_async_remote_copy(
        src_ref=src, dst_ref=dst, send_sem=send, recv_sem=recv, device_id=peer, device_id_type=MESH
    )


def block_of(full, rep, dp, rows, cols):
    if len(full.shape) == 3:
        return full.at[rep, pl.ds(pl.multiple_of(dp * rows, rows), rows)]
    return full.at[pl.ds(pl.multiple_of(rep * rows, rows), rows), pl.ds(pl.multiple_of(dp * cols, cols), cols)]


def half_of(full, rep, rows):
    if len(full.shape) == 3:
        return full.at[rep]
    return full.at[pl.ds(pl.multiple_of(rep * rows, rows), rows)]


def gather_ticks(shard, full, send, recv):
    me = Place()
    rows, cols = shard.shape
    blk = lambda rep, dp: block_of(full, rep, dp, rows, cols)
    rep_y = me.rep + me.dy
    src = lambda k: shard if k == 0 else blk(me.rep, me.from_plane(k))
    own = lambda k: blk(me.rep, me.from_plane(k))
    z_copy = lambda k: remote(shard, own(0), send.at[k - 1], recv.at[k - 1], me.to_plane(k))
    z_land = lambda k: remote(own(k), own(k), send.at[k - 1], recv.at[k - 1], me.to_plane(k))
    x_copy = lambda k: remote(src(k), own(k), send.at[3 + k], recv.at[3 + k], me.across_x)
    y_copy = lambda k: remote(src(k), own(k), send.at[7 + k], recv.at[7 + k], me.across_y)
    x_spot = lambda k: blk(me.rep, me.from_plane(k) + me.dx)
    y_spot = lambda k: blk(rep_y, me.from_plane(k))
    d_spot = lambda k: blk(rep_y, me.from_plane(k) + me.dx)
    x_land = lambda k: remote(x_spot(k), x_spot(k), send.at[3 + k], recv.at[3 + k], me.across_x)
    y_land = lambda k: remote(y_spot(k), y_spot(k), send.at[7 + k], recv.at[7 + k], me.across_y)
    d_land = lambda k: remote(d_spot(k), d_spot(k), send.at[11 + k], recv.at[11 + k], me.across_x)

    def d_copy(k):
        spot = blk(me.rep + (1 - me.c) * me.dy, me.from_plane(k) + me.c * me.dx)
        peer = (me.dp + (1 - me.c) * me.dx, me.rep + me.c * me.dy)
        return remote(spot, spot, send.at[11 + k], recv.at[11 + k], peer)

    mine = (half_of(full, me.rep, rows), half_of(full, rep_y, rows))
    theirs = (half_of(full, me.rep + me.dc, rows), half_of(full, rep_y + me.dc, rows))
    c_copy = lambda j: remote(mine[j], mine[j], send.at[15 + j], recv.at[15 + j], me.other_core)
    c_land = lambda j: remote(theirs[j], theirs[j], send.at[15 + j], recv.at[15 + j], me.other_core)
    place = lambda: pltpu.make_async_copy(shard, own(0), send.at[17])

    def begin():
        x_copy(0).start()
        y_copy(0).start()
        for k in (1, 3, 2):
            z_copy(k).start()
        place().start()

    def spread(k):
        z_land(k).wait_recv()
        x_copy(k).start()
        y_copy(k).start()

    def forward(k):
        x_land(k).wait_recv()
        y_land(k).wait_recv()
        d_copy(k).start()

    def swap():
        place().wait()
        for k in range(4):
            d_land(k).wait_recv()
        for j in range(2):
            c_copy(j).start()

    def end():
        for j in range(2):
            c_land(j).wait_recv()
        for k in range(4):
            if k:
                z_copy(k).wait_send()
            x_copy(k).wait_send()
            y_copy(k).wait_send()
            d_copy(k).wait_send()
        for j in range(2):
            c_copy(j).wait_send()

    def both(a, b):
        def run():
            spread(a)
            forward(b)
        return run

    return begin, [both(1, 0), both(3, 1), both(2, 3), lambda: forward(2), swap], end


class Gather:
    def __init__(self, shards):
        self.shards = list(shards)
        self.count = len(self.shards)

    def shapes(self):
        out = []
        for name, a in self.shards:
            rows, cols = a.shape
            shape = (4 * rows, 8 * cols) if name == "contract" else (4, 8 * rows, cols)
            out.append(jax.ShapeDtypeStruct(shape, a.dtype))
        return out

    def arrays(self):
        return [a for _, a in self.shards]

    def scratch(self):
        return [pltpu.SemaphoreType.DMA((max(self.count, 1), SEMS))] * 2 if self.count else []

    def plan(self, shards, fulls, sems):
        if not self.count:
            return (lambda: None), [], (lambda: None)
        parts = [gather_ticks(s, f, sems[0].at[i], sems[1].at[i]) for i, (s, f) in enumerate(zip(shards, fulls))]

        def begin():
            Place().greet()
            for part in parts:
                part[0]()

        def end():
            for part in parts:
                part[2]()

        return begin, [tick for part in parts for tick in part[1]], end


def scatter_ticks(g, parts, out, send, recv):
    held, other, diag, near, far, planes = parts
    me = Place()
    first = (me.dp + (1 - me.c) * me.dx, me.rep + me.c * me.dy)
    second = (me.dp + me.c * me.dx, me.rep + (1 - me.c) * me.dy)
    flip_y, flip_x = 1 - 2 * me.y, me.dx
    at_first = (me.y + me.c * flip_y, me.x + (1 - me.c) * flip_x)
    at_second = (me.y + (1 - me.c) * flip_y, me.x + me.c * flip_x)
    at_diag = (me.y + flip_y, me.x + flip_x)
    c_copy = lambda j: remote(g.at[2 * j + 1 - me.c], other.at[j], send.at[j], recv.at[j], me.other_core)
    load = lambda j: pltpu.make_async_copy(g.at[2 * j + me.c], held.at[j], send.at[2 + j])
    region = lambda at: held.at[at[0], :, at[1]]
    diag_copy = remote(region(at_diag), diag, send.at[4], recv.at[4], first)
    near_copy = remote(region(at_first), near, send.at[5], recv.at[5], first)
    far_copy = remote(region(at_second), far, send.at[6], recv.at[6], second)
    z_copy = lambda k: remote(
        held.at[me.y, (me.z + k) % 4, me.x], planes.at[k - 1], send.at[6 + k], recv.at[6 + k], me.to_plane(k)
    )

    def add(spot, *terms):
        total = held[spot].astype(F32)
        for ref, i in terms:
            total = total + ref[i].astype(F32)
        held[spot] = total.astype(held.dtype)

    def begin():
        for j in range(2):
            c_copy(j).start()
            load(j).start()

    def fold(j):
        def run():
            c_copy(j).wait_recv()
            load(j).wait()

            @pl.loop(0, 4)
            def _(zz):
                for xx in range(2):
                    add((j, zz, xx), (other, (j, zz, xx)))

            if j == 1:
                diag_copy.start()
                near_copy.start()
        return run

    def pass_on():
        diag_copy.wait_recv()

        @pl.loop(0, 4)
        def _(zz):
            add((at_second[0], zz, at_second[1]), (diag, zz))

        far_copy.start()

    def planes_out():
        near_copy.wait_recv()
        far_copy.wait_recv()

        @pl.loop(0, 4)
        def _(zz):
            add((me.y, zz, me.x), (near, zz), (far, zz))

        for k in (1, 3, 2):
            z_copy(k).start()

    def finish():
        total = held[me.y, me.z, me.x].astype(F32)
        for k in (1, 2, 3):
            z_copy(k).wait_recv()
            total = total + planes[k - 1].astype(F32)
        out[...] = total

    def end():
        for j in range(2):
            c_copy(j).wait_send()
        diag_copy.wait_send()
        near_copy.wait_send()
        far_copy.wait_send()
        for k in (1, 2, 3):
            z_copy(k).wait_send()

    return begin, [fold(0), fold(1), pass_on, planes_out, finish], end


class Scatter:
    def __init__(self, grads):
        self.grads = list(grads)
        self.count = len(self.grads)

    def out_shapes(self):
        return [jax.ShapeDtypeStruct(g.shape[3:], F32) for g in self.grads]

    def scratch(self):
        out = []
        for g in self.grads:
            a, b = g.shape[3:]
            for shape in ((2, 4, 2, a, b), (2, 4, 2, a, b), (4, a, b), (4, a, b), (4, a, b), (3, a, b)):
                out.append(pltpu.VMEM(shape, g.dtype))
        if self.count:
            out += [pltpu.SemaphoreType.DMA((self.count, 10))] * 2
        return out

    def plan(self, grads, outs, scratch):
        if not self.count:
            return (lambda: None), [], (lambda: None)
        send, recv = scratch[-2:]
        parts = [
            scatter_ticks(g, scratch[6 * i : 6 * i + 6], o, send.at[i], recv.at[i])
            for i, (g, o) in enumerate(zip(grads, outs))
        ]

        def begin():
            Place().greet()
            for part in parts:
                part[0]()

        def end():
            for part in parts:
                part[2]()

        order = sorted(
            ((i * 2 + s, i, s) for i in range(len(parts)) for s in range(5))
        )
        return begin, [parts[i][1][s] for _, i, s in order], end


def run_at(step, sub, subs, steps, first, ticks):
    points = steps * subs - first
    for s in range(steps):
        chosen = [t for i, t in enumerate(ticks) if first + min(i * points // max(len(ticks), 1), points - 1) == s * subs + sub]
        if chosen:
            @pl.when(step == s)
            def _():
                for t in chosen:
                    t()


def call(name, body, steps, ticked, subs, first, inputs, outputs, scratch, comm, number):
    gathers = isinstance(comm, Gather)
    extra_in = comm.arrays() if gathers else comm.grads
    extra_out = comm.shapes() if gathers else comm.out_shapes()
    count = comm.count

    def kernel(*refs):
        cut, at = [], 0
        for size in (len(inputs), count, len(outputs), count, len(scratch)):
            cut.append(refs[at : at + size])
            at += size
        ins, c_in, outs, c_out, own = cut
        step = pl.program_id(0)
        begin, ticks, end = comm.plan(c_in, c_out, refs[at:])
        if count:
            pl.when(step == 0)(begin)
        body(step, lambda sub: run_at(step, sub, subs, ticked, first, ticks), ins, outs, own)
        if count:
            pl.when(step == steps - 1)(end)

    return pl.pallas_call(
        kernel,
        grid=(steps,),
        in_specs=[spec for _, spec in inputs] + [ANY] * count,
        out_specs=[spec for _, spec in outputs] + [ANY if gathers else whole(s.shape) for s in extra_out],
        out_shape=[shape for shape, _ in outputs] + extra_out,
        scratch_shapes=scratch + comm.scratch(),
        compiler_params=params(number if count else None),
        name=name,
    )(*[a for a, _ in inputs], *extra_in)


def full(a):
    return a, whole(a.shape)


def shape_of(*dims, dtype=BF):
    return jax.ShapeDtypeStruct(dims, dtype)


def prep_body(step, tick, ins, outs, own):
    base, base_t, marks = ins
    bias, bias_t, mask, mask_t = outs
    n = bias.shape[1]
    tick(0)
    for src, dst in ((base, bias), (base_t, bias_t)):
        row = jnp.broadcast_to(src[0], (n, 2 * n))
        dst[0] = pltpu.roll(row, 0, 1, stride=1, stride_axis=0)[:, :n]

    @pl.when(step == 0)
    def _():
        rows = marks[...]
        seg_r, perm_r, pred_r = rows[0:1], rows[1:2], rows[2:3]
        for lo in range(0, n, 128):
            at = slice(lo, lo + 128)

            def col(k):
                piece = jnp.broadcast_to(rows[k : k + 1, at], (128, 128))
                return piece.T[:, :1]

            seg_c, perm_c, pred_c = col(0), col(1), col(2)
            same = (seg_c == seg_r) & (seg_r != 6.0)
            shown = pred_r == 0.0
            mask[0, at, :] = jnp.where(same & (shown | (perm_r <= perm_c)), 0.0, NEG)
            mask[1, at, :] = jnp.where(same & (shown | (perm_r < perm_c)), 0.0, NEG)
            same = (seg_c == seg_r) & (seg_c != 6.0)
            shown = pred_c == 0.0
            mask_t[at, :n] = jnp.where(same & (shown | (perm_c <= perm_r)), 0.0, NEG)
            mask_t[at, n:] = jnp.where(same & (shown | (perm_c < perm_r)), 0.0, NEG)


def prep(base, base_t, marks, comm, number):
    heads, n2 = base.shape
    n = n2 // 2
    row = pl.BlockSpec((1, 1, n2), lambda h: (h, 0, 0))
    grid = pl.BlockSpec((1, n, n), lambda h: (h, 0, 0))
    return call(
        "prep", prep_body, heads, heads, 1, 1,
        [(base.reshape(heads, 1, n2), row), (base_t.reshape(heads, 1, n2), row), full(marks)],
        [
            (shape_of(heads, n, n, dtype=F32), grid), (shape_of(heads, n, n, dtype=F32), grid),
            (shape_of(2, n, n, dtype=F32), whole((2, n, n))), (shape_of(n, n2, dtype=F32), whole((n, n2))),
        ],
        [], comm, number,
    )


def bias_bases(buckets, bias_table, n):
    selector = (buckets[:, None] == jnp.arange(bias_table.shape[0], dtype=jnp.int32)[None, :]).astype(F32)
    per_offset = jnp.dot(selector, bias_table.astype(F32), precision=lax.Precision.HIGHEST).T * LOG2E
    heads = per_offset.shape[0]
    zero = jnp.zeros((heads, 1), F32)
    base = jnp.concatenate([per_offset[:, n - 1 :], zero, per_offset[:, : n - 1]], axis=1)
    flipped = per_offset[:, ::-1]
    base_t = jnp.concatenate([flipped[:, n - 1 :], zero, flipped[:, : n - 1]], axis=1)
    return selector, base, base_t


def attn_fwd_body(step, tick, ins, outs, own):
    x, y, pw, vec, bias, mask = ins
    q_o, k_o, v_o, ctx_o, lse_o = outs
    pf, lse_s = own
    n, d = x.shape
    pairs = d // 128
    rows_at = n // 2
    p = step

    @pl.when(p == 0)
    def _():
        pf[...] = jnp.concatenate([pw[r] for r in range(pw.shape[0])], axis=1)
        bq, bv = vec[0:1], vec[1:2]
        xv = x[...]
        qc = nn(xv, pf[:, :d]) + bq
        qq = nn(y[...], pf[:, :d]) + bq
        kk = nn(xv, pf[:, d : 2 * d])
        vv = nn(xv, pf[:, 2 * d :]) + bv
        for c in range(pairs):
            at = slice(128 * c, 128 * c + 128)
            q_o[c, :n] = qc[:, at].astype(BF)
            q_o[c, n:] = qq[:, at].astype(BF)
            k_o[c] = kk[:, at].astype(BF)
            v_o[c] = vv[:, at].astype(BF)
        lse_s[...] = jnp.zeros_like(lse_s)

    k = k_o[p]
    v = v_o[p]
    lane = lax.broadcasted_iota(jnp.int32, (1, 128), 1)
    low = lane < 64
    vx = jnp.concatenate([v, jnp.ones_like(v)], axis=1)
    k0 = jnp.where(low, k, 0)
    k1 = jnp.where(low, 0, k)
    for s in range(2):
        for lo in range(0, n, rows_at):
            tick(2 * s + lo // rows_at)
            at = slice(lo, lo + rows_at)
            to = slice(s * n + lo, s * n + lo + rows_at)
            q = q_o[p, to]
            parts = []
            for hh, kh in ((0, k0), (1, k1)):
                sc = nt(q, kh) * (0.125 * LOG2E) + (bias[hh, at] + mask[s, at])
                m = jnp.maximum(jnp.max(sc, axis=-1, keepdims=True), FLOOR)
                e = jnp.exp2(sc - m).astype(BF)
                r = nn(e, vx)
                tot = r[:, 128:]
                tot = jnp.where(tot > 0, tot, 1.0)
                lse = m + jnp.log2(tot)
                lse_s[to] = jnp.where(lane == 2 * p + hh, lse, lse_s[to])
                parts.append(r[:, :128] / tot)
            ctx_o[0, to] = jnp.where(low, parts[0], parts[1]).astype(BF)

    @pl.when(p == pairs - 1)
    def _():
        for lo in range(0, 2 * n, 128):
            lse_o[:, lo : lo + 128] = lse_s[lo : lo + 128].T[: lse_o.shape[0]]


def attn_fwd(x, y, pw, vec, bias, mask, comm, number):
    n, d = x.shape
    pairs = d // 128
    return call(
        "attn_fwd", attn_fwd_body, pairs, pairs, 4, 2,
        [full(x), full(y), full(pw), full(vec), (bias, pl.BlockSpec((2, n, n), lambda p: (p, 0, 0))), full(mask)],
        [
            (shape_of(pairs, 2 * n, 128), whole((pairs, 2 * n, 128))),
            (shape_of(pairs, n, 128), whole((pairs, n, 128))),
            (shape_of(pairs, n, 128), whole((pairs, n, 128))),
            (shape_of(pairs, 2 * n, 128), pl.BlockSpec((1, 2 * n, 128), lambda p: (p, 0, 0))),
            (shape_of(16, 2 * n, dtype=F32), whole((16, 2 * n))),
        ],
        [pltpu.VMEM((d, 3 * d), BF), pltpu.VMEM((2 * n, 128), F32)],
        comm, number,
    )


def gelu_parts(z):
    e = jnp.exp2(z * z * (-0.5 * LOG2E))
    den = 1.0 + (0.3275911 * 0.7071067811865476) * jnp.abs(z)
    t = pl.reciprocal(den, approx=True)
    t = t * (2.0 - den * t)
    poly = t * (0.127414796 + t * (-0.142248368 + t * (0.7107068705 + t * (-0.7265760135 + t * 0.5307027145))))
    tail = poly * e
    phi = jnp.where(z < 0, tail, 1.0 - tail)
    return z * phi, phi + z * (e * 0.3989422804014327)


def moments(v):
    centered = v - jnp.mean(v, axis=-1, keepdims=True)
    rs = lax.rsqrt(jnp.mean(centered * centered, axis=-1, keepdims=True) + 1e-05)
    return centered * rs, rs


def post_fwd_body(step, tick, ins, outs, own):
    x, y, ctx, ow, ew, ct, vec = ins
    rc_o, rq_o, xh1_o, nl_o, act_o, gp_o, xh2_o, rs_o = outs
    (of,) = own
    t = step
    d = x.shape[1]
    fw = ew.shape[2]
    blocks = ew.shape[0] // 2

    @pl.when(t == 0)
    def _():
        of[...] = jnp.concatenate([ow[r] for r in range(ow.shape[0])], axis=1)

    z = jnp.where(t < blocks, x[...].astype(F32), y[...].astype(F32))
    cx = jnp.concatenate([ctx[c] for c in range(ctx.shape[0])], axis=1)
    first = z + (nn(cx, of[...]) + vec[2:3])
    xh1, rs1 = moments(first)
    normed = xh1 * vec[3:4] + vec[4:5]
    nl = normed.astype(BF)
    xh1_o[...] = xh1.astype(BF)
    nl_o[...] = nl
    second = normed + vec[5:6]
    for f in range(ew.shape[0]):
        tick(f)
        at = slice(f * fw, f * fw + fw)
        h = nn(nl, ew[f]) + vec[8 + f : 9 + f]
        act, gp = gelu_parts(h)
        act = act.astype(BF)
        act_o[:, at] = act
        gp_o[:, at] = gp.astype(BF)
        second = second + nt(act, ct[:, at])
    xh2, rs2 = moments(second)
    xh2_o[...] = xh2.astype(BF)
    lane = lax.broadcasted_iota(jnp.int32, (1, 128), 1)
    rs_o[...] = jnp.where(lane < 64, rs1, rs2)
    res = (xh2 * vec[6:7] + vec[7:8]).astype(BF)

    @pl.when(t < blocks)
    def _():
        rc_o[...] = res

    @pl.when(t >= blocks)
    def _():
        rq_o[...] = res


def post_fwd(x, y, ctx, ow, ew, ct, vec, comm, number):
    n, d = x.shape
    ff = ct.shape[1]
    pairs = ctx.shape[0]
    blocks = ew.shape[0] // 2
    tb = n // blocks
    early = pl.BlockSpec((tb, d), lambda t: (jnp.minimum(t, blocks - 1), 0))
    late = pl.BlockSpec((tb, d), lambda t: (jnp.maximum(t - blocks, 0), 0))
    row = lambda width: pl.BlockSpec((tb, width), lambda t: (t, 0))
    return call(
        "post_fwd", post_fwd_body, 2 * blocks, 2 * blocks, ew.shape[0], 1,
        [
            (x, early), (y, late), (ctx, pl.BlockSpec((pairs, tb, 128), lambda t: (0, t, 0))),
            full(ow), full(ew), full(ct), full(vec),
        ],
        [
            (shape_of(n, d), early), (shape_of(n, d), late), (shape_of(2 * n, d), row(d)), (shape_of(2 * n, d), row(d)),
            (shape_of(2 * n, ff), row(ff)), (shape_of(2 * n, ff), row(ff)), (shape_of(2 * n, d), row(d)),
            (shape_of(2 * n, 128, dtype=F32), row(128)),
        ],
        [pltpu.VMEM((d, d), BF)],
        comm, number,
    )


def norm_back(g, xh, rs, gain):
    a = g * gain
    return rs * (a - jnp.mean(a, axis=-1, keepdims=True) - xh * jnp.mean(a * xh, axis=-1, keepdims=True))


def rowsum(v):
    return jnp.sum(v, axis=0, keepdims=True)


def post_bwd_body(step, tick, ins, outs, own):
    gc, gq, ctx, xh1, nl, gp, xh2, rs, act, ow, ew, ct, vec = ins
    first_o, gctx_o, vg_o, do_o, de_o, dc_o = outs
    of, gh_s, nl_t, gf_t, cx_t, ga_s = own
    t = step
    tb, d = gc.shape
    chunks, fw = ew.shape[0], ew.shape[2]
    blocks = chunks // 2

    @pl.when(t == 0)
    def _():
        of[...] = jnp.concatenate([ow[r] for r in range(ow.shape[0])], axis=1)
        vg_o[...] = jnp.zeros_like(vg_o)

    tick(0)

    @pl.when(t < 2 * blocks)
    def _():
        g = jnp.where(t < blocks, gc[...].astype(F32), gq[...].astype(F32))
        rs1, rs2 = rs[:, :1], rs[:, 64:65]
        xh = xh2[...].astype(F32)
        vg_o[6:7] += rowsum(g * xh)
        vg_o[7:8] += rowsum(g)
        gs = norm_back(g, xh, rs2, vec[6:7])
        gf = gs.astype(BF)
        vg_o[5:6] += rowsum(gf.astype(F32))
        gn = gs
        spot = pl.ds(pl.multiple_of(t * tb, tb), tb)
        for f in range(chunks):
            at = slice(f * fw, f * fw + fw)
            gh = (nn(gf, ct[:, at]) * gp[:, at].astype(F32)).astype(BF)
            gh_s[f, spot] = gh
            vg_o[8 + f : 9 + f] += rowsum(gh.astype(F32))
            gn = gn + nt(gh, ew[f])
        xh = xh1[...].astype(F32)
        vg_o[3:4] += rowsum(gn * xh)
        vg_o[4:5] += rowsum(gn)
        first = norm_back(gn, xh, rs1, vec[3:4])
        first_o[...] = first
        ga = first.astype(BF)
        vg_o[2:3] += rowsum(ga.astype(F32))
        ga_s[spot] = ga
        gx = nt(ga, of[...]).astype(BF)
        cx = jnp.concatenate([ctx[c] for c in range(ctx.shape[0])], axis=1)
        for c in range(ctx.shape[0]):
            gctx_o[c] = gx[:, 128 * c : 128 * c + 128]
        nl_t[:, spot] = nl[...].T
        gf_t[:, spot] = gf.T
        cx_t[:, spot] = cx.T

    @pl.when(t == 2 * blocks)
    def _():
        do = nn(cx_t[...], ga_s[...])
        w = do_o.shape[2]
        for r in range(do_o.shape[0]):
            do_o[r] = do[:, r * w : r * w + w].astype(BF)

    @pl.when(t >= 2 * blocks)
    def _():
        de_o[0] = nn(nl_t[...], gh_s[t - 2 * blocks]).astype(BF)
        dc = nn(gf_t[...], act[...]).astype(BF)
        if len(dc_o.shape) == 2:
            dc_o[...] = dc
        else:
            reps, across, a, b = dc_o.shape
            for r in range(reps):
                for x in range(across):
                    dc_o[r, x] = dc[a * r : a * r + a, b * x : b * x + b]


def post_bwd(gc, gq, ctx, xh1, nl, gp, xh2, rs, act, ow, ew, ct, vec, comm, number, split):
    n, d = gc.shape
    chunks, fw = ew.shape[0], ew.shape[2]
    ff = chunks * fw
    pairs = ctx.shape[0]
    blocks = chunks // 2
    tb = n // blocks
    last = 2 * blocks - 1
    tok = lambda width: pl.BlockSpec((tb, width), lambda t: (jnp.minimum(t, last), 0))
    tok3 = pl.BlockSpec((pairs, tb, 128), lambda t: (0, jnp.minimum(t, last), 0))
    part = lambda t: jnp.maximum(t - last - 1, 0)
    if split:
        reps, owners = split
        across = owners // chunks
        dc = (
            shape_of(reps, owners, d // reps, ff // owners),
            pl.BlockSpec((reps, across, d // reps, ff // owners), lambda t: (0, part(t), 0, 0)),
        )
    else:
        dc = shape_of(d, ff), pl.BlockSpec((d, fw), lambda t: (0, part(t)))
    return call(
        "post_bwd", post_bwd_body, 2 * blocks + chunks, 2 * blocks + chunks, 1, 1,
        [
            (gc, pl.BlockSpec((tb, d), lambda t: (jnp.minimum(t, blocks - 1), 0))),
            (gq, pl.BlockSpec((tb, d), lambda t: (jnp.clip(t - blocks, 0, blocks - 1), 0))),
            (ctx, tok3), (xh1, tok(d)), (nl, tok(d)), (gp, tok(ff)), (xh2, tok(d)), (rs, tok(128)),
            (act, pl.BlockSpec((2 * n, fw), lambda t: (0, part(t)))),
            full(ow), full(ew), full(ct), full(vec),
        ],
        [
            (shape_of(2 * n, d, dtype=F32), tok(d)), (shape_of(pairs, 2 * n, 128), tok3),
            (shape_of(16, d, dtype=F32), whole((16, d))), (shape_of(*ow.shape), whole(ow.shape)),
            (shape_of(chunks, d, fw), pl.BlockSpec((1, d, fw), lambda t: (part(t), 0, 0))), dc,
        ],
        [
            pltpu.VMEM((d, d), BF), pltpu.VMEM((chunks, 2 * n, fw), BF),
            pltpu.VMEM((d, 2 * n), BF), pltpu.VMEM((d, 2 * n), BF), pltpu.VMEM((d, 2 * n), BF),
            pltpu.VMEM((2 * n, d), BF),
        ],
        comm, number,
    )


def attn_bwd_body(step, tick, ins, outs, own):
    q, k, v, go, lse, bias_t, mask_t, x, y, first, pw = ins
    gx_o, gy_o, dp_o, bg_o, t8_o = outs
    pf, dq_s, dk_s, dv_s, diag, x_t, dk_a, dv_a = own
    p = step
    n, d = x.shape
    pairs = d // 128
    wide = diag.shape[2]
    cols = n // 2

    @pl.when(p == 0)
    def _():
        pf[...] = jnp.concatenate([pw[r] for r in range(pw.shape[0])], axis=1)
        x_t[:, :n] = x[...].T
        x_t[:, n:] = y[...].T

    @pl.when(p < pairs)
    def _():
        low = lax.broadcasted_iota(jnp.int32, (1, 128), 1) < 64
        only = lambda a, hh: jnp.where(low, a, 0) if hh == 0 else jnp.where(low, 0, a)
        diag[...] = jnp.zeros_like(diag)
        ka, va = k[0], v[0]
        for i, lo in enumerate(range(0, 2 * n, cols)):
            tick(i)
            at = slice(lo, lo + cols)
            i0 = lo % n
            qa, ga = q[0, at], go[0, at]
            dq = dk = dv = None
            for hh in range(2):
                km, vm = only(ka, hh), only(va, hh)
                lrow = lse[pl.ds(2 * p + hh, 1), at]
                sc = nt(km, qa) * (0.125 * LOG2E) + (bias_t[hh, :, i0 : i0 + cols] + mask_t[:, at])
                pr = jnp.exp2(sc - lrow)
                gp = nt(vm, ga)
                ds = pr * (gp - rowsum(pr * gp))
                dsb = ds.astype(BF)
                dv_h = nn(pr.astype(BF), only(ga, hh))
                dk_h = nn(dsb, only(qa, hh))
                dq_h = tn(dsb, km)
                dq, dk, dv = (dq_h, dk_h, dv_h) if hh == 0 else (dq + dq_h, dk + dk_h, dv + dv_h)
                for b in range(n // 128):
                    off = n - 128 - 128 * b + i0
                    diag[hh, :, off : off + cols] += ds[128 * b : 128 * b + 128]
            dq_s[p, at] = (dq * 0.125).astype(BF)
            if i == 0:
                dk_a[...] = dk
                dv_a[...] = dv
            else:
                dk_a[...] += dk
                dv_a[...] += dv
        dk_s[p] = (dk_a[...] * 0.125).astype(BF)
        dv_s[p] = dv_a[...].astype(BF)
        for hh in range(2):
            total = jnp.zeros((8, 2 * n), F32)
            for g in range(16):
                piece = jnp.concatenate([diag[hh, 8 * g : 8 * g + 8], jnp.zeros((8, 2 * n - wide), F32)], axis=1)
                total = total + (pltpu.roll(piece, 2 * n - 8 * g, 1) if g else piece)
            t8_o[hh] = total

    @pl.when(p == pairs)
    def _():
        cat = lambda ref, at: jnp.concatenate([ref[c, at] for c in range(pairs)], axis=1)
        gqc, gqq = cat(dq_s, slice(0, n)), cat(dq_s, slice(n, 2 * n))
        gk, gv = cat(dk_s, slice(0, n)), cat(dv_s, slice(0, n))
        gx_o[...] = first[:n] + nt(gqc, pf[:, :d]) + nt(gk, pf[:, d : 2 * d]) + nt(gv, pf[:, 2 * d :])
        gy_o[...] = first[n:] + nt(gqq, pf[:, :d])
        bg_o[...] = jnp.zeros_like(bg_o)
        bg_o[0:1] = rowsum(gqc.astype(F32)) + rowsum(gqq.astype(F32))
        bg_o[1:2] = rowsum(gv.astype(F32))
        xt = x_t[:, :n]
        grads = jnp.concatenate([
            nn(x_t[...], jnp.concatenate([gqc, gqq], axis=0)).astype(BF),
            nn(xt, gk).astype(BF), nn(xt, gv).astype(BF)], axis=1)
        w = dp_o.shape[2]
        for r in range(dp_o.shape[0]):
            dp_o[r] = grads[:, r * w : r * w + w]


def attn_bwd(q, k, v, go, lse, bias_t, mask_t, x, y, first, pw, comm, number):
    n, d = x.shape
    pairs = d // 128
    pair = lambda *block: pl.BlockSpec(block, lambda p: (jnp.minimum(p, pairs - 1), 0, 0))
    return call(
        "attn_bwd", attn_bwd_body, pairs + 1, pairs, 4, 2,
        [
            (q, pair(1, 2 * n, 128)), (k, pair(1, n, 128)), (v, pair(1, n, 128)), (go, pair(1, 2 * n, 128)),
            full(lse), (bias_t, pair(2, n, n)), full(mask_t), full(x), full(y), full(first), full(pw),
        ],
        [
            (shape_of(n, d, dtype=F32), whole((n, d))), (shape_of(n, d, dtype=F32), whole((n, d))),
            (shape_of(*pw.shape), whole(pw.shape)), (shape_of(8, d, dtype=F32), whole((8, d))),
            (shape_of(2 * pairs, 8, 2 * n, dtype=F32), pair(2, 8, 2 * n)),
        ],
        [
            pltpu.VMEM((d, 3 * d), BF), pltpu.VMEM((pairs, 2 * n, 128), BF),
            pltpu.VMEM((pairs, n, 128), BF), pltpu.VMEM((pairs, n, 128), BF),
            pltpu.VMEM((2, 128, 2 * n - 128), F32), pltpu.VMEM((d, 2 * n), BF),
            pltpu.VMEM((n, 128), F32), pltpu.VMEM((n, 128), F32),
        ],
        comm, number,
    )


def offset_sums(t8, n):
    total = sum(jnp.roll(t8[:, r], -(n - 128 + r), axis=1) for r in range(t8.shape[1]))
    return jnp.concatenate([total[:, 1:n][:, ::-1], total[:, :1], total[:, n + 1 :][:, ::-1]], axis=1)


def tail_kernel(comm, *refs):
    count = comm.count
    ins, outs, scratch = refs[:count], refs[count : 2 * count], refs[2 * count :]
    begin, ticks, end = comm.plan(ins, outs, scratch)
    begin()
    for tick in ticks:
        tick()
    end()


def tail(comm, number):
    return pl.pallas_call(
        functools.partial(tail_kernel, comm),
        in_specs=[ANY] * comm.count,
        out_specs=[pl.BlockSpec(memory_space=pltpu.VMEM)] * comm.count,
        out_shape=comm.out_shapes(),
        scratch_shapes=comm.scratch(),
        compiler_params=params(number),
        name="tail",
    )(*comm.grads)


NAMES = ("project", "output", "expand", "contract")


def vector_block(vectors):
    rows, cols = vectors.shape
    return jnp.pad(vectors, ((0, 8 - rows), (0, 128 - cols)))


def vectors_whole(gathered, lo, rows, cols):
    part = gathered.reshape(4, 8, 16, 128)[:, :, lo : lo + rows, :cols]
    return part.transpose(0, 2, 1, 3).reshape(4 * rows, 8 * cols).astype(F32)


def plain_gather(project, output, expand, contract, vectors):
    rows = lambda a, dim: lax.all_gather(a, "dp", axis=dim, tiled=True)
    pw = lax.all_gather(rows(project, 0), "rep", axis=0)
    ow = lax.all_gather(rows(output, 0), "rep", axis=0)
    ew = lax.all_gather(rows(expand, 0), "rep", axis=0)
    ct = lax.all_gather(rows(contract, 1), "rep", axis=0, tiled=True)
    vec = lax.all_gather(rows(vectors, 1), "rep", axis=0, tiled=True).astype(F32)
    return pw, ow, ew, ct, vec


def scatter_sum(a, rep_dim, dp_dim):
    a = lax.psum_scatter(a, "rep", scatter_dimension=rep_dim, tiled=True)
    return lax.psum_scatter(a, "dp", scatter_dimension=dp_dim, tiled=True).astype(F32)


def shards(
    square,
    content_stream, query_stream, segments, perm_order, predicted, buckets, bias_table,
    project_one, output_one, expand_one, contract_one, vectors_one,
    project_two, output_two, expand_two, contract_two, vectors_two,
    content_cotangent, query_cotangent,
):
    shape = content_stream.shape
    n, d = shape[1:]
    flat = lambda a: a.reshape(n, d)
    selector, base, base_t = bias_bases(buckets, bias_table, n)
    marks = jnp.concatenate([segments, perm_order, predicted, jnp.zeros((5, n), jnp.int32)]).astype(F32)
    one = (project_one, output_one, expand_one, contract_one.T, vectors_one)
    two = (project_two, output_two, expand_two, contract_two.T, vectors_two)
    none = Gather([])
    pick = lambda weights, names: Gather([(k, weights[NAMES.index(k)]) for k in names])
    x, y = flat(content_stream), flat(query_stream)
    ins = [(x, y)]
    if square:
        rows, cols = vectors_one.shape
        both = jnp.concatenate([vector_block(vectors_one), vector_block(vectors_two)], axis=0)
        bias, bias_t, mask, mask_t, pw, vecs = prep(
            base, base_t, marks, Gather([("project", project_one), ("vectors", both)]), 1
        )
        vec_one, vec_two = (vectors_whole(vecs, lo, rows, cols) for lo in (0, 8))
        *att_one, ow, ew, ct = attn_fwd(x, y, pw, vec_one, bias, mask, pick(one, NAMES[1:]), 2)
        full_one = (pw, ow, ew, ct, vec_one)
        *post_one, pw, ow = post_fwd(x, y, att_one[3], ow, ew, ct, vec_one, pick(two, NAMES[:2]), 3)
        x, y = post_one[:2]
        ins.append((x, y))
        *att_two, ew, ct = attn_fwd(x, y, pw, vec_two, bias, mask, pick(two, NAMES[2:]), 4)
        full_two = (pw, ow, ew, ct, vec_two)
        post_two = post_fwd(x, y, att_two[3], ow, ew, ct, vec_two, none, 0)
    else:
        bias, bias_t, mask, mask_t = prep(base, base_t, marks, none, 0)
        full_one, full_two = plain_gather(*one), plain_gather(*two)
        pw, ow, ew, ct, vec = full_one
        att_one = attn_fwd(x, y, pw, vec, bias, mask, none, 0)
        post_one = post_fwd(x, y, att_one[3], ow, ew, ct, vec, none, 0)
        x, y = post_one[:2]
        ins.append((x, y))
        pw, ow, ew, ct, vec = full_two
        att_two = attn_fwd(x, y, pw, vec, bias, mask, none, 0)
        post_two = post_fwd(x, y, att_two[3], ow, ew, ct, vec, none, 0)

    def back_post(gx, gy, weights, att, post, comm, number):
        pw, ow, ew, ct, vec = weights
        xh1, nl, act, gp, xh2, rs = post[2:]
        split = (4, 8) if square else None
        return post_bwd(gx, gy, att[3], xh1, nl, gp, xh2, rs, act, ow, ew, ct, vec, comm, number, split)

    def back_attn(gctx, first, weights, att, inputs, comm, number):
        q, k, v, ctx, lse = att
        return attn_bwd(q, k, v, gctx, lse, bias_t, mask_t, *inputs, first, weights[0], comm, number)

    empty = Scatter([])
    pieces = lambda a: a.reshape(4, 4, 2, a.shape[-2] if a.ndim == 4 else a.shape[1] // 8, a.shape[-1])
    sent = lambda *arrays: Scatter([pieces(a) for a in arrays]) if square else empty
    first, gctx, vg_two, do_two, de_two, dc_two, *_ = back_post(
        flat(content_cotangent), flat(query_cotangent), full_two, att_two, post_two, empty, 0
    )
    gx, gy, dp_two, bg_two, t8_two, *out_two = back_attn(
        gctx, first, full_two, att_two, ins[1], sent(do_two, de_two, dc_two), 5
    )
    first, gctx, vg_one, do_one, de_one, dc_one, *out_p2 = back_post(
        gx, gy, full_one, att_one, post_one, sent(dp_two), 6
    )
    gx, gy, dp_one, bg_one, t8_one, *out_one = back_attn(
        gctx, first, full_one, att_one, ins[0], sent(do_one, de_one, dc_one), 7
    )
    vg_one = jnp.concatenate([bg_one[:2], vg_one[2:12]], axis=0)
    vg_two = jnp.concatenate([bg_two[:2], vg_two[2:12]], axis=0)
    distances = offset_sums(t8_one + t8_two, n)
    table = jnp.dot(selector.T, distances.T, precision=lax.Precision.HIGHEST)
    table = lax.psum(table, ("dp", "rep"))
    if square:
        vgs = jnp.stack([vg_one, vg_two]).reshape(2, 4, rows, 8, cols).transpose(1, 3, 0, 2, 4)
        vgs = jnp.pad(vgs.reshape(4, 8, 2 * rows, cols), ((0, 0), (0, 0), (0, 8 - 2 * rows), (0, 128 - cols)))
        out_p1, vecs = tail(Scatter([pieces(dp_one), pieces(vgs)]), 8)
        grads_one = (out_p1, out_one[0], out_one[1], out_one[2].T, vecs[:rows, :cols])
        grads_two = (out_p2[0], out_two[0], out_two[1], out_two[2].T, vecs[rows : 2 * rows, :cols])
    else:
        spread = lambda dp, do, de, dc, vec: (
            scatter_sum(dp, 0, 1)[0], scatter_sum(do, 0, 1)[0], scatter_sum(de, 0, 1)[0],
            scatter_sum(dc, 0, 1).T, scatter_sum(vec, 0, 1),
        )
        grads_one = spread(dp_one, do_one, de_one, dc_one, vg_one)
        grads_two = spread(dp_two, do_two, de_two, dc_two, vg_two)
    return (
        post_two[0].reshape(shape), post_two[1].reshape(shape), gx.reshape(shape), gy.reshape(shape), table,
        *grads_one, *grads_two,
    )


def solution(mesh):
    rows3, rows2 = P(("dp", "rep"), None, None), P(("dp", "rep"), None)
    weights = (P("dp", "rep"),) * 4 + (P("rep", "dp"),)
    square = mesh.shape["dp"] == 8 and mesh.shape["rep"] == 4
    return jax.shard_map(
        functools.partial(shards, square),
        mesh=mesh,
        in_specs=(rows3, rows3, rows2, rows2, rows2, P(), P(), *weights, *weights, rows3, rows3),
        out_specs=(rows3, rows3, rows3, rows3, P(), *weights, *weights),
        check_vma=False,
    )
```

time: 1700 us -> 664 us (0.39)
  waiting for transfers between devices: 1150 us -> 0 us
  Pallas kernels: 267 us -> 594 us
  blocking collectives: 225 us -> 38.7 us
    reduce_scatter x14 -> x0, waiting for transfers between devices: 728 us -> none  [the longest x6 383 us: scatter_sum(): lax.psum_scatter(a, 'dp', scatter_dimension=dp_dim, tiled=True).astype(F32)]
    pallas_call x9 -> x10, Pallas kernels: 267 us -> 594 us  [the longest x9 550 us: call(): pl.pallas_call(kernel, grid=(steps,), in_specs=[spec for _, spec in input...]
    unnamed x36 -> x0, waiting for transfers between devices: 253 us -> none
    all_gather x8 -> x0, blocking collectives: 186 us -> none  [the longest x6 175 us: gather_layer(): rows = lambda a, dim: lax.all_gather(a, 'dp', axis=dim, tiled=True)]
    all_gather x12 -> x0, waiting for transfers between devices: 169 us -> none  [the longest x2 78 us: gather_layer(): ct = lax.all_gather(rows(contract.T, 1), 'rep', axis=0, tiled=True)]
  transfers between devices with their start and end apart: 31 -> 0, of which waited for: 27 -> 0; matrix products, arithmetic and copies ran while one was open for 2% -> 0% of each run, Pallas kernels for 5% -> 0%
where the time goes in v2:
time: 664 us; the launch traced here: 657 us
  Pallas kernels  594 us (89%)
  blocking collectives  38.7 us (6%)
  local copies, waits for them, and re-layouts  17.8 us (3%)
    pallas_call x9, Pallas kernels, call(): pl.pallas_call(kernel, grid=(steps,), in_specs=[spec for _, spec in input...  550 us
    pallas_call x1, Pallas kernels, tail(): pl.pallas_call(functools.partial(tail_kernel, comm), in_specs=[ANY] * com...  43.6 us
    psum x1, blocking collectives, shards(): table = lax.psum(table, ('dp', 'rep'))  38.7 us

profile of v2, /device:TPU:0, one launch (start us, length us, event | category | flops | bytes accessed | tf_op | source)
XLA Modules:
  0.0 657.2 jit_solution(18366872838678554577)
XLA Ops:
  0.7 1.3 fusion.16.refs_4_
  2.0 1.4 add_convert_fusion.refs_2_
  3.4 1.0 broadcast_multiply_fusion.1
  6.7 43.0 %prep.1 = (f32[12,512,512]{2,1,0:T(8,128)}, f32[12,512,512]{2,1,0:T(8,128)}, f32[2,512,512]{2,1,0:T(8,128)}, f32[512,1024]{1,0:T(8,128)}, bf16[4,768,576]{2,1,0:T(8,128)(2,1)}, /*index=5*/bf16[4,128,128]{2,1,0:T(8,128)(2,1)}) custom-call(f32[12,1,1024]{2,1,0:T(1,128)} %copy.45.refs_0_, f32[12,1,1024]{2,1,0:T(1,128)} %reshape.109.refs_1_, ...), custom_call_target="tpu_custom_call" | custom-call | tf_op jit(solution)/shard_map/prep/pallas_call | solution.py:359
  49.7 0.9 fusion.19
  52.1 74.0 %attn_fwd.2 = (bf16[6,1024,128]{2,1,0:T(8,128)(2,1)}, bf16[6,512,128]{2,1,0:T(8,128)(2,1)}, bf16[6,512,128]{2,1,0:T(8,128)(2,1)}, bf16[6,1024,128]{2,1,0:T(8,128...) custom-call(bf16[512,768]{1,0:T(8,128)(2,1)} %bitcast.68, ...), custom_call_target="tpu_custom_call" | custom-call | tf_op jit(solution)/shard_map/attn_fwd/pallas_call | solution.py:359
  126.0 54.7 %post_fwd.2 = (bf16[512,768]{1,0:T(8,128)(2,1)}, bf16[512,768]{1,0:T(8,128)(2,1)}, bf16[1024,768]{1,0:T(8,128)(2,1)}, bf16[1024,768]{1,0:T(8,128)(2,1)}, bf16[10...) custom-call(bf16[512,768]{1,0:T(8,128)(2,1)} %bitcast.69, ...), custom_call_target="tpu_custom_call" | custom-call | tf_op jit(solution)/shard_map/post_fwd/pallas_call | solution.py:359
  180.7 65.8 %attn_fwd.3 = (bf16[6,1024,128]{2,1,0:T(8,128)(2,1)}, bf16[6,512,128]{2,1,0:T(8,128)(2,1)}, bf16[6,512,128]{2,1,0:T(8,128)(2,1)}, bf16[6,1024,128]{2,1,0:T(8,128...) custom-call(bf16[512,768]{1,0:T(8,128)(2,1)} %get-tuple-element.93.refs_0_.refs_7_, ...), custom_call_target="tpu_custom_call" | custom-call | tf_op jit(solution)/shard_map/attn_fwd/pallas_call | solution.py:359
  246.6 30.9 %post_fwd.3 = (bf16[512,768]{1,0:T(8,128)(2,1)}, bf16[512,768]{1,0:T(8,128)(2,1)}, bf16[1024,768]{1,0:T(8,128)(2,1)}, bf16[1024,768]{1,0:T(8,128)(2,1)}, bf16[10...) custom-call(bf16[512,768]{1,0:T(8,128)(2,1)} %get-tuple-element.93.refs_0_.re, ...), custom_call_target="tpu_custom_call" | custom-call | tf_op jit(solution)/shard_map/post_fwd/pallas_call | solution.py:359
  277.4 37.5 %post_bwd.2 = (f32[1024,768]{1,0:T(8,128)}, bf16[6,1024,128]{2,1,0:T(8,128)(2,1)}, f32[16,768]{1,0:T(8,128)}, bf16[4,768,192]{2,1,0:T(8,128)(2,1)}, bf16[4,768,7...) custom-call(bf16[512,768]{1,0:T(8,128)(2,1)} %bitcast.84, bf16[512,768]{1,0:T(8,128)(2,1)} %bitcast.85, ...), custom_call_target="tpu_custom_call" | custom-call | tf_op jit(solution)/shard_map/post_bwd/pallas_call | solution.py:359
  315.0 94.0 %attn_bwd.2 = (f32[512,768]{1,0:T(8,128)}, f32[512,768]{1,0:T(8,128)}, bf16[4,768,576]{2,1,0:T(8,128)(2,1)}, f32[8,768]{1,0:T(8,128)}, f32[12,8,1024]{2,1,0:T(8,...) custom-call(bf16[6,1024,128]{2,1,0:T(8,128)(2,1)} %get-tuple-element.105.refs_0_, ...), custom_call_target="tpu_custom_call" | custom-call | tf_op jit(solution)/shard_map/attn_bwd/pallas_call | solution.py:359
  409.0 56.5 %post_bwd.3 = (f32[1024,768]{1,0:T(8,128)}, bf16[6,1024,128]{2,1,0:T(8,128)(2,1)}, f32[16,768]{1,0:T(8,128)}, bf16[4,768,192]{2,1,0:T(8,128)(2,1)}, bf16[4,768,7...) custom-call(f32[512,768]{1,0:T(8,128)} %get-tuple-element.122.refs_0_, ...), custom_call_target="tpu_custom_call" | custom-call | tf_op jit(solution)/shard_map/post_bwd/pallas_call | solution.py:359
  465.5 93.6 %attn_bwd.3 = (f32[512,768]{1,0:T(8,128)}, f32[512,768]{1,0:T(8,128)}, bf16[4,768,576]{2,1,0:T(8,128)(2,1)}, f32[8,768]{1,0:T(8,128)}, f32[12,8,1024]{2,1,0:T(8,...) custom-call(bf16[6,1024,128]{2,1,0:T(8,128)(2,1)} %get-tuple-element.102.refs_0_, ...), custom_call_target="tpu_custom_call" | custom-call | tf_op jit(solution)/shard_map/attn_bwd/pallas_call | solution.py:359
  559.2 1.1 add.32
  560.5 0.7 slice.166
  561.2 0.7 slice.168
  563.1 43.6 %tail.1 = (f32[96,576]{1,0:T(8,128)}, f32[8,128]{1,0:T(8,128)}) custom-call(bf16[4,4,2,96,576]{4,3,2,1,0:T(8,128)(2,1)} %bitcast.78, f32[4,4,2,8,128]{4,3,2,1,0:T(8,128)} %bitcast.86), custom_call_target="tpu_custom_call" | custom-call | tf_op jit(solution)/shard_map/tail/pallas_call | solution.py:842
  606.7 1.4 fusion.21
  610.2 38.7 %psum.7 = f32[32,12]{0,1:T(8,128)} all-reduce(f32[32,12]{0,1:T(8,128)S(1)} %fusion), channel_id=1, replica_groups=mesh['dp'=8,'rep'=4] {'dp','rep'}, use_global_device_ids=true, to_apply=%region_0.1 | all-reduce | flops 384 | bytes 3072 | tf_op jit(solution)/shard_map/psum | solution.py:955
  648.8 1.1 copy.97
  650.0 1.1 copy.98
  652.5 0.7 copy.101
  653.2 0.7 copy.102
  656.0 0.7 copy.106
  (94 shorter events, 10.4 us)
Async XLA Ops:
  0.6 2.8 copy-start
  465.5 93.6 %copy-start.4 = (f32[12,8,1024]{2,1,0:T(8,128)S(1)}, f32[12,8,1024]{2,1,0:T(8,128)}, u32[]{:S(2)}) copy-start(f32[12,8,1024]{2,1,0:T(8,128)} %get-tuple-element.140) | copy-start | bytes 1179652
  559.1 2.9 copy-start.14
  559.1 3.1 copy-start.13
  606.7 3.1 copy-start.15
  606.7 42.1 %copy-start.3 = (f32[512,768]{1,0:T(8,128)S(1)}, f32[512,768]{1,0:T(8,128)}, u32[]{:S(2)}) copy-start(f32[512,768]{1,0:T(8,128)} %get-tuple-element.137) | copy-start | bytes 4718596
  608.7 41.2 %copy-start.2 = (f32[512,768]{1,0:T(8,128)S(1)}, f32[512,768]{1,0:T(8,128)}, u32[]{:S(2)}) copy-start(f32[512,768]{1,0:T(8,128)} %get-tuple-element.138) | copy-start | bytes 4718596
  650.0 1.2 copy-start.10
  650.0 1.9 copy-start.12
  650.0 2.5 copy-start.8
  650.0 3.3 copy-start.7
  650.0 4.0 copy-start.9
  650.0 4.7 copy-start.11
  650.0 5.3 copy-start.6
  650.0 6.7 %copy-start.1 = (bf16[32,12]{0,1:T(8,128)(2,1)S(1)}, bf16[32,12]{0,1:T(8,128)(2,1)}, u32[]{:S(2)}) copy-start(bf16[32,12]{0,1:T(8,128)(2,1)} %param.25) | copy-start | bytes 2308
  651.2 4.8 copy-start.5
